TPU v7x, 32 devices: a whole 2x2x4 slice. The times are simulated.
32 devices in a mesh: tm: 32 (over z, y, x, core).
Axes of the slice: x: 2, y: 2, z: 4, core: 2. Of those that a mesh axis runs over, the one named last changes fastest.
Arguments:
- transition: float32 [256, 128, 128], P('tm'), may hold values from -0.5 to 1
- obs_precision: float32 [256, 128], P('tm'), may hold values from 0.0001 to 0.001
- observations: float32 [256, 128], P('tm'), may hold values from -12 to 12
Outputs:
- smoothed: float32 [256, 128], P('tm')
All inputs are finite; a program needn't handle non-finite values.
Results may differ from a plain program's by a relative error of at most 0.0004.
Values sent between devices are 32-bit elements; how exact they have to be, the bound alone decides.
No kernel may reach another device: no remote copies, remote signals or barrier semaphores. Data moves between devices by JAX's collectives and lax.ppermute only.
A program may use at most 64 MiB of HBM per device.

v0:
```python
import functools

import jax
import jax.numpy as jnp
from jax import lax
from jax.experimental import pallas as pl
from jax.experimental.pallas import tpu as pltpu
from jax.sharding import PartitionSpec as P

HIGHEST = lax.Precision.HIGHEST
PANEL = 16
ROWS = 8
SIDE_BY_SIDE = 4


def dot(left, right, contract=((1,), (0,))):
    return lax.dot_general(
        left, right, (contract, ((), ())), precision=HIGHEST, preferred_element_type=jnp.float32
    )


def spread(row):
    return jnp.broadcast_to(row, (ROWS, row.shape[1]))


def lane(tile, column):
    return jnp.broadcast_to(tile[:, column : column + 1], tile.shape)


def summed(terms):
    while len(terms) > 1:
        pairs = [terms[i] + terms[i + 1] for i in range(0, len(terms) - 1, 2)]
        terms = pairs + terms[len(pairs) * 2 :]
    return terms[0]


def panel_solved(cols, rows, masks):
    tiles = len(rows)
    scale = [None] * tiles
    for j in range(len(cols)):
        h, s = divmod(j, ROWS)
        inv = 1.0 / spread(cols[j][h][s : s + 1])
        scale[h] = inv if scale[h] is None else jnp.where(masks[s], inv, scale[h])
        factor = [cols[j][g] * inv for g in range(tiles)]
        factor[h] = jnp.where(masks[s], 0.0, factor[h])
        for c in range(j + 1, len(cols)):
            top = spread(cols[c][h][s : s + 1])
            for g in range(tiles):
                cols[c][g] = cols[c][g] - factor[g] * top
        top = spread(rows[h][s : s + 1])
        for g in range(tiles):
            rows[g] = rows[g] - factor[g] * top
    return [rows[g] * scale[g] for g in range(tiles)]


def inverses(matrices, ahead):
    n = matrices[0].shape[0]
    b = PANEL
    tiles = b // ROWS
    matrices = list(matrices)
    sub_id = lax.broadcasted_iota(jnp.int32, (ROWS, n), 0)
    lane_id = lax.broadcasted_iota(jnp.int32, (ROWS, n), 1)
    full_lane = lax.broadcasted_iota(jnp.int32, (n, n), 1)
    masks = [sub_id == j for j in range(ROWS)]

    def tiled(m, start):
        return [m[start + g * ROWS : start + (g + 1) * ROWS] for g in range(tiles)]

    panels = [tiled(m, 0) for m in matrices]
    for start in range(0, n, b):
        end = start + b
        in_panel = (lane_id >= start) & (lane_id < end)
        in_full = (full_lane >= start) & (full_lane < end)
        ready = []
        for panel in panels:
            cols = [[lane(panel[g], start + c) for g in range(tiles)] for c in range(b)]
            rows = [
                jnp.where(
                    in_panel, jnp.where(lane_id - start == sub_id + ROWS * g, 1.0, 0.0), panel[g]
                )
                for g in range(tiles)
            ]
            ready.append((cols, rows))
        solved = [panel_solved(cols, rows, masks) for cols, rows in ready]
        for q, m in enumerate(matrices):
            if ahead and end < n:
                panels[q] = [
                    jnp.where(in_panel, 0.0, t)
                    - summed(
                        [
                            lane(t, start + j) * spread(solved[q][j // ROWS][j % ROWS : j % ROWS + 1])
                            for j in range(b)
                        ]
                    )
                    for t in tiled(m, end)
                ]
            whole = jnp.concatenate(solved[q], axis=0)
            rest = jnp.where(in_full, 0.0, m) - dot(m[:, start:end], whole)
            parts = [rest[:start]] if start else []
            parts.append(whole)
            if end < n:
                if ahead:
                    parts += panels[q]
                    if end + b < n:
                        parts.append(rest[end + b :])
                else:
                    parts.append(rest[end:])
                    panels[q] = tiled(rest, end)
            matrices[q] = jnp.concatenate(parts, axis=0)
    return matrices


def eliminated(inverse, sources):
    z = dot(sources, inverse)
    return z, dot(z, sources[: sources.shape[0] - ROWS], ((1,), (1,)))


def padded(row):
    return jnp.concatenate([row, jnp.zeros((ROWS - 1, row.shape[1]), jnp.float32)], axis=0)


def write_element(out_ref, n, alpha, gamma, beta, u, v):
    out_ref[0:n] = alpha
    out_ref[n : 2 * n] = gamma
    out_ref[2 * n : 3 * n] = beta
    out_ref[3 * n : 3 * n + ROWS] = jnp.concatenate(
        [u, v, jnp.zeros((ROWS - 2, n), jnp.float32)], axis=0
    )


def bit_of(axis, level):
    return lax.rem(lax.div(lax.axis_index(axis), 2**level), 2)


def local_kernel(
    trans_hbm, prec_hbm, obs_hbm, elem_ref, z_ref,
    prec_ref, obs_ref, center_ref, inv_ref, fwd_ref, bwd_ref, vec_ref, sems,
):
    steps, n = prec_ref.shape
    always = lax.axis_index("tm") >= 0
    small = [
        pltpu.make_async_copy(prec_hbm, prec_ref, sems.at[steps]),
        pltpu.make_async_copy(obs_hbm, obs_ref, sems.at[steps + 1]),
    ]
    large = [
        pltpu.make_async_copy(trans_hbm.at[t], fwd_ref.at[t], sems.at[t]) for t in range(steps)
    ]
    for copy in small + large:
        copy.start()
    for copy in small:
        copy.wait()

    @pl.when(always)
    def _():
        row_id = lax.broadcasted_iota(jnp.int32, (n, n), 0)
        lane_id = lax.broadcasted_iota(jnp.int32, (n, n), 1)
        for t in range(steps):
            large[t].wait()
            a = fwd_ref[t]
            scale = 1.0 + prec_ref[t : t + 1, :]
            center_ref[t] = jnp.where(row_id == lane_id, scale, 0.0) + dot(a, a, ((0,), (0,)))
            if t % 2 == 0:
                bwd_ref[t] = a.T
        center_ref[steps] = jnp.zeros((n, n), jnp.float32)
        vec_ref[0:steps] = prec_ref[...] * obs_ref[...]
        vec_ref[steps : steps + 1] = jnp.zeros((1, n), jnp.float32)

    slot = 0
    gap = 1
    while gap < steps:
        odd = list(range(gap, steps, 2 * gap))
        for first in range(0, len(odd), SIDE_BY_SIDE):
            group = odd[first : first + SIDE_BY_SIDE]

            @pl.when(always)
            def _(group=group):
                for j, inverse in zip(group, inverses([center_ref[j] for j in group], len(group) <= 2)):
                    inv_ref[j] = inverse

        @pl.when(always)
        def _(odd=odd, gap=gap, slot=slot):
            for k, j in enumerate(odd):
                low, high = j - gap, j + gap
                sources = jnp.concatenate(
                    [bwd_ref[low], fwd_ref[j], padded(vec_ref[j : j + 1])], axis=0
                )
                z, gram = eliminated(inv_ref[j], sources)
                z_ref[slot + k] = z
                center_ref[low] = center_ref[low] - gram[0:n, 0:n]
                center_ref[high] = center_ref[high] - gram[n : 2 * n, n : 2 * n]
                vec_ref[low : low + 1] = vec_ref[low : low + 1] + gram[2 * n : 2 * n + 1, 0:n]
                vec_ref[high : high + 1] = (
                    vec_ref[high : high + 1] + gram[2 * n : 2 * n + 1, n : 2 * n]
                )
                fwd_ref[low] = gram[n : 2 * n, 0:n]
                bwd_ref[low] = gram[0:n, n : 2 * n]

        slot += len(odd)
        gap *= 2
    beta = jnp.where(bit_of("tm", 0) == 0, bwd_ref[0], fwd_ref[0])
    write_element(
        elem_ref, n, center_ref[0], center_ref[steps], beta, vec_ref[0:1], vec_ref[steps : steps + 1]
    )


def merge_parts(level, mine_ref, theirs_ref):
    n = mine_ref.shape[1]
    is_left = bit_of("tm", level) == 0

    def part(lo, hi):
        m, t = mine_ref[lo:hi], theirs_ref[lo:hi]
        return jnp.where(is_left, m, t), jnp.where(is_left, t, m)

    alpha_l, alpha_r = part(0, n)
    gamma_l, gamma_r = part(n, 2 * n)
    beta_l, beta_r = part(2 * n, 3 * n)
    vec_l, vec_r = part(3 * n, 3 * n + ROWS)
    (inverse,) = inverses([alpha_r + gamma_l], True)
    target = vec_r[0:1] + vec_l[1:2]
    z, gram = eliminated(inverse, jnp.concatenate([beta_l, beta_r, padded(target)], axis=0))
    alpha = alpha_l - gram[0:n, 0:n]
    gamma = gamma_r - gram[n : 2 * n, n : 2 * n]
    u = vec_l[0:1] + gram[2 * n : 2 * n + 1, 0:n]
    v = vec_r[1:2] + gram[2 * n : 2 * n + 1, n : 2 * n]
    return z, alpha, gamma, gram[n : 2 * n, 0:n], gram[0:n, n : 2 * n], u, v


def merge_kernel(level, mine_ref, theirs_ref, elem_ref, z_ref):
    n = mine_ref.shape[1]
    z, alpha, gamma, beta, beta_t, u, v = merge_parts(level, mine_ref, theirs_ref)
    z_ref[...] = z
    chosen = jnp.where(bit_of("tm", level + 1) == 0, beta_t, beta)
    write_element(elem_ref, n, alpha, gamma, chosen, u, v)


def closing_kernel(level, mine_ref, theirs_ref, small_ref, z_ref, first_ref):
    n = mine_ref.shape[1]
    z, alpha, gamma, beta, _, u, v = merge_parts(level, mine_ref, theirs_ref)
    z_ref[...] = z
    (inverse,) = inverses([alpha], True)
    first = dot(jnp.concatenate([beta, padded(u)], axis=0), inverse)
    first_ref[...] = first
    gram = dot(first, beta, ((1,), (1,)))
    is_lower = bit_of("tm", level + 1) == 0
    small_ref[0:n] = jnp.where(is_lower, gamma - gram[0:n], alpha)
    small_ref[n : n + ROWS] = padded(jnp.where(is_lower, v + gram[n : n + 1], u))


def between(z, low, high):
    n = low.shape[1]
    return z[2 * n : 2 * n + 1] + dot(jnp.concatenate([low, high], axis=1), z[0 : 2 * n])


def final_kernel(levels, steps, *refs):
    mine_ref, theirs_ref = refs[0:2]
    z_refs = refs[2 : levels + 1]
    first_ref, local_ref, out_ref = refs[levels + 1 :]
    n = mine_ref.shape[1]
    (inverse,) = inverses([mine_ref[0:n] + theirs_ref[0:n]], True)
    middle = dot(mine_ref[n : n + 1] + theirs_ref[n : n + 1], inverse)
    first = first_ref[n : n + 1] + dot(middle, first_ref[0:n])
    is_lower = bit_of("tm", levels - 1) == 0
    low = jnp.where(is_lower, first, middle)
    high = jnp.where(is_lower, middle, 0.0)
    for level in range(levels - 2, -1, -1):
        middle = between(z_refs[level], low, high)
        is_left = bit_of("tm", level) == 0
        low, high = jnp.where(is_left, low, middle), jnp.where(is_left, middle, high)
    states = {0: low, steps: high}
    slot = steps - 1
    gap = steps
    while gap > 1:
        slot -= steps // gap
        for k, start in enumerate(range(0, steps, gap)):
            states[start + gap // 2] = between(
                local_ref.at[slot + k], states[start], states[start + gap]
            )
        gap //= 2
    out_ref[...] = jnp.concatenate([states[t] for t in range(steps)], axis=0)


def body(transition, obs_precision, observations):
    steps, n = obs_precision.shape
    devices = lax.axis_size("tm")
    levels = devices.bit_length() - 1
    params = pltpu.CompilerParams(vmem_limit_bytes=48 * 2**20)
    element = jax.ShapeDtypeStruct((3 * n + ROWS, n), jnp.float32)
    z_shape = jax.ShapeDtypeStruct((2 * n + ROWS, n), jnp.float32)
    mine, local_z = pl.pallas_call(
        local_kernel,
        out_shape=(element, jax.ShapeDtypeStruct((steps - 1,) + z_shape.shape, jnp.float32)),
        in_specs=[pl.BlockSpec(memory_space=pl.ANY)] * 3,
        scratch_shapes=[
            pltpu.VMEM((steps, n), jnp.float32),
            pltpu.VMEM((steps, n), jnp.float32),
            pltpu.VMEM((steps + 1, n, n), jnp.float32),
            pltpu.VMEM((steps, n, n), jnp.float32),
            pltpu.VMEM((steps, n, n), jnp.float32),
            pltpu.VMEM((steps, n, n), jnp.float32),
            pltpu.VMEM((2 * steps, n), jnp.float32),
            pltpu.SemaphoreType.DMA((steps + 2,)),
        ],
        compiler_params=params,
        name="local",
    )(transition, obs_precision, observations)
    zs = []
    small = jax.ShapeDtypeStruct((n + ROWS, n), jnp.float32)

    def exchanged(array, level):
        return lax.ppermute(array, "tm", [(i, i ^ 2**level) for i in range(devices)])

    for level in range(levels - 2):
        mine, z = pl.pallas_call(
            functools.partial(merge_kernel, level),
            out_shape=(element, z_shape),
            compiler_params=params,
            name="merge",
        )(mine, exchanged(mine, level))
        zs.append(z)
    last, z, first = pl.pallas_call(
        functools.partial(closing_kernel, levels - 2),
        out_shape=(small, z_shape, small),
        compiler_params=params,
        name="closing",
    )(mine, exchanged(mine, levels - 2))
    return pl.pallas_call(
        functools.partial(final_kernel, levels, steps),
        out_shape=jax.ShapeDtypeStruct((steps, n), jnp.float32),
        compiler_params=params,
        name="final",
    )(last, exchanged(last, levels - 1), *zs, z, first, local_z)


def solution(mesh):
    return jax.shard_map(
        body,
        mesh=mesh,
        in_specs=(P("tm", None, None), P("tm", None), P("tm", None)),
        out_specs=P("tm", None),
        check_vma=False,
    )
```

profile of v0, /device:TPU:0, one launch (start us, length us, event | category | flops | bytes accessed | tf_op | source)
XLA Modules:
  0.0 75.5 jit_solution(9664132733207569989)
XLA Ops:
  0.0 0.0 copy-start
  0.0 1.0 %copy-done = f32[8,128,128]{2,1,0:T(8,128)S(1)} copy-done((f32[8,128,128]{2,1,0:T(8,128)S(1)}, f32[8,128,128]{2,1,0:T(8,128)}, u32[]{:S(2)}) %copy-start) | copy-done | bytes 524312
  1.0 0.0 copy-start.1
  1.0 0.7 copy-done.1
  1.7 0.0 copy-start.2
  1.7 0.7 copy-done.2
  2.4 20.8 %local.1 = (f32[392,128]{1,0:T(8,128)S(1)}, f32[7,264,128]{2,1,0:T(8,128)S(1)}) custom-call(f32[8,128,128]{2,1,0:T(8,128)S(1)} %copy-done, f32[8,128]{1,0:T(8,128)S(1)} %copy-done.1, f32[8,128]{1,0:T(8,128)S(1)} %copy-done.2), custom_call_target="tpu_custom_call" | custom-call | tf_op jit(solution)/shard_map/local/pallas_call | solution.py:289
  23.3 0.5 collective-permute-start
  23.8 1.1 %collective-permute-done.theirs_ref = f32[392,128]{1,0:T(8,128)S(1)} collective-permute-done((f32[392,128]{1,0:T(8,128)S(1)}, f32[392,128]{1,0:T(8,128)S(1)}, u32[]{:S(2)}, u32[]{:S(2)}) %collective-permute-start) | collective-permute-done | bytes 200736 | tf_op jit(solution)/shard_map/ppermute | solution.py:310
  24.9 3.9 %merge.3 = (f32[392,128]{1,0:T(8,128)S(1)}, f32[264,128]{1,0:T(8,128)S(1)}) custom-call(f32[392,128]{1,0:T(8,128)S(1)} %get-tuple-element.16.mine_ref, f32[392,128]{1,0:T(8,128)S(1)} %collective-permute-done.theirs_ref), custom_call_target="tpu_custom_call" | custom-call | tf_op jit(solution)/shard_map/merge/pallas_call | solution.py:313
  28.8 2.9 %collective-permute-start.1 = (f32[392,128]{1,0:T(8,128)S(1)}, f32[392,128]{1,0:T(8,128)S(1)}, u32[]{:S(2)}, u32[]{:S(2)}) collective-permute-start(f32[392,128]{1,0:T(8,128)S(1)} %get-tuple-element.17.mine_ref), channel_id=1, source_target_pairs={{0,2},{1,3},{2,0},{3,1},{4,6},{5,7},{6,4},{7,5},{8,10},{9,11},{10,... | collective-permute-start | bytes 602120 | tf_op jit(solution)/shard_map/ppermute | solution.py:310
  31.7 5.3 %collective-permute-done.1.theirs_ref = f32[392,128]{1,0:T(8,128)S(1)} collective-permute-done((f32[392,128]{1,0:T(8,128)S(1)}, f32[392,128]{1,0:T(8,128)S(1)}, u32[]{:S(2)}, u32[]{:S(2)}) %collective-permute-start.1) | collective-permute-done | bytes 200736 | tf_op jit(solution)/shard_map/ppermute | solution.py:310
  37.0 3.9 %merge.4 = (f32[392,128]{1,0:T(8,128)S(1)}, f32[264,128]{1,0:T(8,128)S(1)}) custom-call(f32[392,128]{1,0:T(8,128)S(1)} %get-tuple-element.17.mine_ref, f32[392,128]{1,0:T(8,128)S(1)} %collective-permute-done.1.theirs_ref), custom_call_target="tpu_custom_call" | custom-call | tf_op jit(solution)/shard_map/merge/pallas_call | solution.py:313
  41.0 1.8 %collective-permute-start.2 = (f32[392,128]{1,0:T(8,128)S(1)}, f32[392,128]{1,0:T(8,128)S(1)}, u32[]{:S(2)}, u32[]{:S(2)}) collective-permute-start(f32[392,128]{1,0:T(8,128)S(1)} %get-tuple-element.18.mine_ref), channel_id=1, source_target_pairs={{0,4},{1,5},{2,6},{3,7},{4,0},{5,1},{6,2},{7,3},{8,12},{9,13},{10,... | collective-permute-start | bytes 602120 | tf_op jit(solution)/shard_map/ppermute | solution.py:310
  42.8 4.8 %collective-permute-done.2.theirs_ref = f32[392,128]{1,0:T(8,128)S(1)} collective-permute-done((f32[392,128]{1,0:T(8,128)S(1)}, f32[392,128]{1,0:T(8,128)S(1)}, u32[]{:S(2)}, u32[]{:S(2)}) %collective-permute-start.2) | collective-permute-done | bytes 200736 | tf_op jit(solution)/shard_map/ppermute | solution.py:310
  47.6 3.9 %merge.5 = (f32[392,128]{1,0:T(8,128)S(1)}, f32[264,128]{1,0:T(8,128)S(1)}) custom-call(f32[392,128]{1,0:T(8,128)S(1)} %get-tuple-element.18.mine_ref, f32[392,128]{1,0:T(8,128)S(1)} %collective-permute-done.2.theirs_ref), custom_call_target="tpu_custom_call" | custom-call | tf_op jit(solution)/shard_map/merge/pallas_call | solution.py:313
  51.5 1.6 %collective-permute-start.3 = (f32[392,128]{1,0:T(8,128)S(1)}, f32[392,128]{1,0:T(8,128)S(1)}, u32[]{:S(2)}, u32[]{:S(2)}) collective-permute-start(f32[392,128]{1,0:T(8,128)S(1)} %get-tuple-element.19.mine_ref), channel_id=1, source_target_pairs={{0,8},{1,9},{2,10},{3,11},{4,12},{5,13},{6,14},{7,15},{8,0},{9,1},... | collective-permute-start | bytes 602120 | tf_op jit(solution)/shard_map/ppermute | solution.py:310
  53.1 4.2 %collective-permute-done.3.theirs_ref = f32[392,128]{1,0:T(8,128)S(1)} collective-permute-done((f32[392,128]{1,0:T(8,128)S(1)}, f32[392,128]{1,0:T(8,128)S(1)}, u32[]{:S(2)}, u32[]{:S(2)}) %collective-permute-start.3) | collective-permute-done | bytes 200736 | tf_op jit(solution)/shard_map/ppermute | solution.py:310
  57.3 7.7 %closing.1 = (f32[136,128]{1,0:T(8,128)S(1)}, f32[264,128]{1,0:T(8,128)S(1)}, f32[136,128]{1,0:T(8,128)S(1)}) custom-call(f32[392,128]{1,0:T(8,128)S(1)} %get-tuple-element.19.mine_ref, f32[392,128]{1,0:T(8,128)S(1)} %collective-permute-done.3.theirs_ref), custom_call_target="tpu_custom_call" | custom-call | tf_op jit(solution)/shard_map/closing/pallas_call | solution.py:320
  65.0 2.6 %collective-permute-start.4 = (f32[136,128]{1,0:T(8,128)S(1)}, f32[136,128]{1,0:T(8,128)S(1)}, u32[]{:S(2)}, u32[]{:S(2)}) collective-permute-start(f32[136,128]{1,0:T(8,128)S(1)} %get-tuple-element.20.refs_0_), channel_id=1, source_target_pairs={{0,16},{1,17},{2,18},{3,19},{4,20},{5,21},{6,22},{7,23},{8,24},{9,... | collective-permute-start | bytes 208904 | tf_op jit(solution)/shard_map/ppermute | solution.py:310
  67.6 2.7 %collective-permute-done.4.refs_1_ = f32[136,128]{1,0:T(8,128)S(1)} collective-permute-done((f32[136,128]{1,0:T(8,128)S(1)}, f32[136,128]{1,0:T(8,128)S(1)}, u32[]{:S(2)}, u32[]{:S(2)}) %collective-permute-start.4) | collective-permute-done | bytes 69664 | tf_op jit(solution)/shard_map/ppermute | solution.py:310
  70.3 5.2 %final.1 = f32[8,128]{1,0:T(8,128)} custom-call(f32[136,128]{1,0:T(8,128)S(1)} %get-tuple-element.20.refs_0_, f32[136,128]{1,0:T(8,128)S(1)} %collective-permute-done.4.refs_1_, f32[264,128]{1,0:T(8,128)S(1)} %get-tuple-element.21.refs_2_, f32[264,128]{1,0:T(8,128)S(1)} %get-tuple-element.22.refs_3_, f32[264,128]{1,0:T(8,128)S(1)} %get-tuple-element.23.refs_4_, ...), custom_call_target="tpu_custom_call" | custom-call | tf_op jit(solution)/shard_map/final/pallas_call | solution.py:326
Async XLA Ops:
  0.0 1.0 %copy-start = (f32[8,128,128]{2,1,0:T(8,128)S(1)}, f32[8,128,128]{2,1,0:T(8,128)}, u32[]{:S(2)}) copy-start(f32[8,128,128]{2,1,0:T(8,128)} %trans_hbm.1) | copy-start | bytes 1572868
  1.0 0.7 copy-start.1
  1.7 0.7 copy-start.2
  23.3 1.6 %collective-permute-start = (f32[392,128]{1,0:T(8,128)S(1)}, f32[392,128]{1,0:T(8,128)S(1)}, u32[]{:S(2)}, u32[]{:S(2)}) collective-permute-start(f32[392,128]{1,0:T(8,128)S(1)} %get-tuple-element.16.mine_ref), channel_id=1, source_target_pairs={{0,1},{1,0},{2,3},{3,2},{4,5},{5,4},{6,7},{7,6},{8,9},{9,8},{10,11... | collective-permute-start | bytes 602120 | tf_op jit(solution)/shard_map/ppermute | solution.py:310
  28.8 8.2 %collective-permute-start.1 = (f32[392,128]{1,0:T(8,128)S(1)}, f32[392,128]{1,0:T(8,128)S(1)}, u32[]{:S(2)}, u32[]{:S(2)}) collective-permute-start(f32[392,128]{1,0:T(8,128)S(1)} %get-tuple-element.17.mine_ref), channel_id=1, source_target_pairs={{0,2},{1,3},{2,0},{3,1},{4,6},{5,7},{6,4},{7,5},{8,10},{9,11},{10,... | collective-permute-start | bytes 602120 | tf_op jit(solution)/shard_map/ppermute | solution.py:310
  41.0 6.6 %collective-permute-start.2 = (f32[392,128]{1,0:T(8,128)S(1)}, f32[392,128]{1,0:T(8,128)S(1)}, u32[]{:S(2)}, u32[]{:S(2)}) collective-permute-start(f32[392,128]{1,0:T(8,128)S(1)} %get-tuple-element.18.mine_ref), channel_id=1, source_target_pairs={{0,4},{1,5},{2,6},{3,7},{4,0},{5,1},{6,2},{7,3},{8,12},{9,13},{10,... | collective-permute-start | bytes 602120 | tf_op jit(solution)/shard_map/ppermute | solution.py:310
  51.5 5.8 %collective-permute-start.3 = (f32[392,128]{1,0:T(8,128)S(1)}, f32[392,128]{1,0:T(8,128)S(1)}, u32[]{:S(2)}, u32[]{:S(2)}) collective-permute-start(f32[392,128]{1,0:T(8,128)S(1)} %get-tuple-element.19.mine_ref), channel_id=1, source_target_pairs={{0,8},{1,9},{2,10},{3,11},{4,12},{5,13},{6,14},{7,15},{8,0},{9,1},... | collective-permute-start | bytes 602120 | tf_op jit(solution)/shard_map/ppermute | solution.py:310
  65.0 5.3 %collective-permute-start.4 = (f32[136,128]{1,0:T(8,128)S(1)}, f32[136,128]{1,0:T(8,128)S(1)}, u32[]{:S(2)}, u32[]{:S(2)}) collective-permute-start(f32[136,128]{1,0:T(8,128)S(1)} %get-tuple-element.20.refs_0_), channel_id=1, source_target_pairs={{0,16},{1,17},{2,18},{3,19},{4,20},{5,21},{6,22},{7,23},{8,24},{9,... | collective-permute-start | bytes 208904 | tf_op jit(solution)/shard_map/ppermute | solution.py:310
where the time goes:
time: 75.7 us; the launch traced here: 75.5 us
  Pallas kernels  45.6 us (60%)
  waiting for transfers between devices  18 us (24%)
  starting transfers between devices  9.46 us (12%)
  local copies, waits for them, and re-layouts  2.41 us (3%)
    pallas_call x1, Pallas kernels, body(): pl.pallas_call(local_kernel, out_shape=(element, jax.ShapeDtypeStruct((st...  20.8 us
    ppermute x5, waiting for transfers between devices, exchanged(): lax.ppermute(array, 'tm', [(i, i ^ 2 ** level) for i in range(devices)])  18 us
    pallas_call x3, Pallas kernels, body(): pl.pallas_call(functools.partial(merge_kernel, level), out_shape=(element...  11.8 us
    ppermute x5, starting transfers between devices, exchanged(): lax.ppermute(array, 'tm', [(i, i ^ 2 ** level) for i in range(devices)])  9.46 us
    pallas_call x1, Pallas kernels, body(): pl.pallas_call(functools.partial(closing_kernel, levels - 2), out_shape=(...  7.71 us
    pallas_call x1, Pallas kernels, body(): pl.pallas_call(functools.partial(final_kernel, levels, steps), out_shape=...  5.2 us
    unnamed x6, local copies, waits for them, and re-layouts  2.41 us
  transfers between devices with their start and end apart: 5, of which 5 were waited for; matrix products, arithmetic and copies ran while one was open for 0% of the time, Pallas kernels for 0%

commit v1 on v0

--- a/solution.py
+++ b/solution.py
@@ -119,13 +119,17 @@
     return jnp.concatenate([row, jnp.zeros((ROWS - 1, row.shape[1]), jnp.float32)], axis=0)
 
 
-def write_element(out_ref, n, alpha, gamma, beta, u, v):
-    out_ref[0:n] = alpha
-    out_ref[n : 2 * n] = gamma
-    out_ref[2 * n : 3 * n] = beta
-    out_ref[3 * n : 3 * n + ROWS] = jnp.concatenate(
-        [u, v, jnp.zeros((ROWS - 2, n), jnp.float32)], axis=0
-    )
+def write_near(is_left, near_ref, alpha, gamma, u, v):
+    n = alpha.shape[0]
+    near_ref[0:n] = jnp.where(is_left, gamma, alpha)
+    near_ref[n : n + ROWS] = padded(jnp.where(is_left, v, u))
+
+
+def write_far(is_left, far_ref, alpha, gamma, beta_t, beta, u, v):
+    n = alpha.shape[0]
+    far_ref[0:n] = jnp.where(is_left, alpha, gamma)
+    far_ref[n : 2 * n] = jnp.where(is_left, beta_t, beta)
+    far_ref[2 * n : 2 * n + ROWS] = padded(jnp.where(is_left, u, v))
 
 
 def bit_of(axis, level):
@@ -133,21 +137,19 @@
 
 
 def local_kernel(
-    trans_hbm, prec_hbm, obs_hbm, elem_ref, z_ref,
+    trans_hbm, prec_hbm, obs_hbm, near_ref, far_ref, z_ref,
     prec_ref, obs_ref, center_ref, inv_ref, fwd_ref, bwd_ref, vec_ref, sems,
 ):
     steps, n = prec_ref.shape
     always = lax.axis_index("tm") >= 0
-    small = [
-        pltpu.make_async_copy(prec_hbm, prec_ref, sems.at[steps]),
-        pltpu.make_async_copy(obs_hbm, obs_ref, sems.at[steps + 1]),
+    copies = [
+        pltpu.make_async_copy(trans_hbm, fwd_ref, sems.at[0]),
+        pltpu.make_async_copy(prec_hbm, prec_ref, sems.at[1]),
+        pltpu.make_async_copy(obs_hbm, obs_ref, sems.at[2]),
     ]
-    large = [
-        pltpu.make_async_copy(trans_hbm.at[t], fwd_ref.at[t], sems.at[t]) for t in range(steps)
-    ]
-    for copy in small + large:
+    for copy in copies:
         copy.start()
-    for copy in small:
+    for copy in copies:
         copy.wait()
 
     @pl.when(always)
@@ -155,7 +157,6 @@
         row_id = lax.broadcasted_iota(jnp.int32, (n, n), 0)
         lane_id = lax.broadcasted_iota(jnp.int32, (n, n), 1)
         for t in range(steps):
-            large[t].wait()
             a = fwd_ref[t]
             scale = 1.0 + prec_ref[t : t + 1, :]
             center_ref[t] = jnp.where(row_id == lane_id, scale, 0.0) + dot(a, a, ((0,), (0,)))
@@ -197,45 +198,68 @@
 
         slot += len(odd)
         gap *= 2
-    beta = jnp.where(bit_of("tm", 0) == 0, bwd_ref[0], fwd_ref[0])
-    write_element(
-        elem_ref, n, center_ref[0], center_ref[steps], beta, vec_ref[0:1], vec_ref[steps : steps + 1]
+    is_left = bit_of("tm", 0) == 0
+    alpha, gamma, u, v = center_ref[0], center_ref[steps], vec_ref[0:1], vec_ref[steps : steps + 1]
+    write_near(is_left, near_ref, alpha, gamma, u, v)
+    write_far(is_left, far_ref, alpha, gamma, bwd_ref[0], fwd_ref[0], u, v)
+
+
+def inverse_kernel(near_ref, came_near_ref, inv_ref):
+    n = near_ref.shape[1]
+    inv_ref[...] = inverses([near_ref[0:n] + came_near_ref[0:n]], True)[0]
+
+
+def parts(level, far_ref, came_far_ref):
+    n = far_ref.shape[1]
+    is_left = bit_of("tm", level) == 0
+
+    def part(lo, hi):
+        m, t = far_ref[lo:hi], came_far_ref[lo:hi]
+        return jnp.where(is_left, m, t), jnp.where(is_left, t, m)
+
+    return (*part(0, n), *part(n, 2 * n), *part(2 * n, 2 * n + ROWS))
+
+
+def near_kernel(level, inv_ref, near_ref, came_near_ref, far_ref, came_far_ref, near_out):
+    n = near_ref.shape[1]
+    alpha, gamma, beta_low, beta_high, u, v = parts(level, far_ref, came_far_ref)
+    next_left = bit_of("tm", level + 1) == 0
+    beta = jnp.where(next_left, beta_high, beta_low)
+    target = near_ref[n : n + ROWS] + came_near_ref[n : n + ROWS]
+    gram = dot(
+        dot(jnp.concatenate([beta, target], axis=0), inv_ref[...]), beta, ((1,), (1,))
     )
-
-
-def merge_parts(level, mine_ref, theirs_ref):
-    n = mine_ref.shape[1]
-    is_left = bit_of("tm", level) == 0
-
-    def part(lo, hi):
-        m, t = mine_ref[lo:hi], theirs_ref[lo:hi]
-        return jnp.where(is_left, m, t), jnp.where(is_left, t, m)
-
-    alpha_l, alpha_r = part(0, n)
-    gamma_l, gamma_r = part(n, 2 * n)
-    beta_l, beta_r = part(2 * n, 3 * n)
-    vec_l, vec_r = part(3 * n, 3 * n + ROWS)
-    (inverse,) = inverses([alpha_r + gamma_l], True)
-    target = vec_r[0:1] + vec_l[1:2]
-    z, gram = eliminated(inverse, jnp.concatenate([beta_l, beta_r, padded(target)], axis=0))
-    alpha = alpha_l - gram[0:n, 0:n]
-    gamma = gamma_r - gram[n : 2 * n, n : 2 * n]
-    u = vec_l[0:1] + gram[2 * n : 2 * n + 1, 0:n]
-    v = vec_r[1:2] + gram[2 * n : 2 * n + 1, n : 2 * n]
-    return z, alpha, gamma, gram[n : 2 * n, 0:n], gram[0:n, n : 2 * n], u, v
-
-
-def merge_kernel(level, mine_ref, theirs_ref, elem_ref, z_ref):
-    n = mine_ref.shape[1]
-    z, alpha, gamma, beta, beta_t, u, v = merge_parts(level, mine_ref, theirs_ref)
+    near_out[0:n] = jnp.where(next_left, gamma, alpha) - gram[0:n]
+    near_out[n : n + ROWS] = jnp.where(next_left, v, u) + gram[n : n + ROWS]
+
+
+def merged(level, inv_ref, near_ref, came_near_ref, far_ref, came_far_ref):
+    n = near_ref.shape[1]
+    alpha, gamma, beta_low, beta_high, u, v = parts(level, far_ref, came_far_ref)
+    target = near_ref[n : n + ROWS] + came_near_ref[n : n + ROWS]
+    z, gram = eliminated(inv_ref[...], jnp.concatenate([beta_low, beta_high, target], axis=0))
+    return (
+        z,
+        alpha - gram[0:n, 0:n],
+        gamma - gram[n : 2 * n, n : 2 * n],
+        gram[0:n, n : 2 * n],
+        gram[n : 2 * n, 0:n],
+        u[0:1] + gram[2 * n : 2 * n + 1, 0:n],
+        v[0:1] + gram[2 * n : 2 * n + 1, n : 2 * n],
+    )
+
+
+def far_kernel(level, *refs):
+    far_out, z_ref = refs[6:]
+    z, alpha, gamma, beta_t, beta, u, v = merged(level, *refs[:5])
     z_ref[...] = z
-    chosen = jnp.where(bit_of("tm", level + 1) == 0, beta_t, beta)
-    write_element(elem_ref, n, alpha, gamma, chosen, u, v)
-
-
-def closing_kernel(level, mine_ref, theirs_ref, small_ref, z_ref, first_ref):
-    n = mine_ref.shape[1]
-    z, alpha, gamma, beta, _, u, v = merge_parts(level, mine_ref, theirs_ref)
+    write_far(bit_of("tm", level + 1) == 0, far_out, alpha, gamma, beta_t, beta, u, v)
+
+
+def closing_kernel(level, *refs):
+    small_ref, z_ref, first_ref = refs[5:]
+    z, alpha, gamma, _, beta, u, v = merged(level, *refs[:5])
+    n = alpha.shape[0]
     z_ref[...] = z
     (inverse,) = inverses([alpha], True)
     first = dot(jnp.concatenate([beta, padded(u)], axis=0), inverse)
@@ -284,12 +308,13 @@
     devices = lax.axis_size("tm")
     levels = devices.bit_length() - 1
     params = pltpu.CompilerParams(vmem_limit_bytes=48 * 2**20)
-    element = jax.ShapeDtypeStruct((3 * n + ROWS, n), jnp.float32)
-    z_shape = jax.ShapeDtypeStruct((2 * n + ROWS, n), jnp.float32)
-    mine, local_z = pl.pallas_call(
+    small = jax.ShapeDtypeStruct((n + ROWS, n), jnp.float32)
+    large = jax.ShapeDtypeStruct((2 * n + ROWS, n), jnp.float32)
+    square = jax.ShapeDtypeStruct((n, n), jnp.float32)
+    near, far, local_z = pl.pallas_call(
         local_kernel,
-        out_shape=(element, jax.ShapeDtypeStruct((steps - 1,) + z_shape.shape, jnp.float32)),
-        in_specs=[pl.BlockSpec(memory_space=pl.ANY)] * 3,
+        out_shape=(small, large, jax.ShapeDtypeStruct((steps - 1,) + large.shape, jnp.float32)),
+        in_specs=[pl.BlockSpec(memory_space=pltpu.HBM)] * 3,
         scratch_shapes=[
             pltpu.VMEM((steps, n), jnp.float32),
             pltpu.VMEM((steps, n), jnp.float32),
@@ -298,37 +323,53 @@
             pltpu.VMEM((steps, n, n), jnp.float32),
             pltpu.VMEM((steps, n, n), jnp.float32),
             pltpu.VMEM((2 * steps, n), jnp.float32),
-            pltpu.SemaphoreType.DMA((steps + 2,)),
+            pltpu.SemaphoreType.DMA((3,)),
         ],
-        compiler_params=params,
+        compiler_params=pltpu.CompilerParams(vmem_limit_bytes=60 * 2**20),
         name="local",
     )(transition, obs_precision, observations)
     zs = []
-    small = jax.ShapeDtypeStruct((n + ROWS, n), jnp.float32)
 
     def exchanged(array, level):
         return lax.ppermute(array, "tm", [(i, i ^ 2**level) for i in range(devices)])
 
-    for level in range(levels - 2):
-        mine, z = pl.pallas_call(
-            functools.partial(merge_kernel, level),
-            out_shape=(element, z_shape),
+    def called(kernel, out_shape, name, flops, *arrays):
+        whole = pl.BlockSpec(memory_space=pltpu.VMEM)
+        unread = pl.BlockSpec(memory_space=pl.ANY)
+        return pl.pallas_call(
+            kernel,
+            out_shape=out_shape,
+            in_specs=[whole] * 5 + [unread] if len(arrays) == 6 else [whole] * len(arrays),
             compiler_params=params,
-            name="merge",
-        )(mine, exchanged(mine, level))
+            cost_estimate=pl.CostEstimate(
+                flops=flops, bytes_accessed=12 * n * n, transcendentals=0
+            ),
+            name=name,
+        )(*arrays)
+
+    for level in range(levels - 1):
+        came_near = exchanged(near, level)
+        came_far = exchanged(far, level)
+        inverse = called(inverse_kernel, square, "inverse", 3000 * n**3, near, came_near)
+        held = (inverse, near, came_near, far, came_far)
+        if level < levels - 2:
+            near = called(
+                functools.partial(near_kernel, level), small, "near", 500 * n**3, *held
+            )
+            far, z = called(
+                functools.partial(far_kernel, level), (large, large), "far", 700 * n**3, *held, near
+            )
+        else:
+            near, z, first = called(
+                functools.partial(closing_kernel, level), (small, large, small), "closing", 2000 * n**3, *held
+            )
         zs.append(z)
-    last, z, first = pl.pallas_call(
-        functools.partial(closing_kernel, levels - 2),
-        out_shape=(small, z_shape, small),
-        compiler_params=params,
-        name="closing",
-    )(mine, exchanged(mine, levels - 2))
     return pl.pallas_call(
         functools.partial(final_kernel, levels, steps),
         out_shape=jax.ShapeDtypeStruct((steps, n), jnp.float32),
         compiler_params=params,
         name="final",
-    )(last, exchanged(last, levels - 1), *zs, z, first, local_z)
+    )(near, exchanged(near, levels - 1), *zs, first, local_z)
 
 
 def solution(mesh):

time: 75.7 us -> 69.2 us (0.914)
  waiting for transfers between devices: 18 us -> 10.4 us
  local copies, waits for them, and re-layouts: 2.41 us -> 0.89 us
  Pallas kernels: 45.6 us -> 47.1 us
  starting transfers between devices: 9.46 us -> 10.6 us
    ppermute x5 -> x9, waiting for transfers between devices: 18 us -> 10.4 us  [exchanged(): lax.ppermute(array, 'tm', [(i, i ^ 2 ** level) for i in range(devices)])]
    unnamed x6, local copies, waits for them, and re-layouts: 2.41 us -> 0.89 us
    pallas_call x5 -> x12, Pallas kernels: 40.4 us -> 41.9 us  [the longest x11 21.5 us: called(): pl.pallas_call(kernel, out_shape=out_shape, in_specs=[whole] * 5 + [unrea...]
    ppermute x5 -> x9, starting transfers between devices: 9.46 us -> 10.6 us  [exchanged(): lax.ppermute(array, 'tm', [(i, i ^ 2 ** level) for i in range(devices)])]
  transfers between devices with their start and end apart: 5 -> 9, of which waited for: 5 -> 6; matrix products, arithmetic and copies ran while one was open for 0% -> 0% of each run, Pallas kernels for 0% -> 22%
where the time goes in v1:
time: 69.2 us; the launch traced here: 69 us
  Pallas kernels  47.1 us (68%)
  starting transfers between devices  10.6 us (15%)
  waiting for transfers between devices  10.4 us (15%)
  local copies, waits for them, and re-layouts  0.89 us (1%)
    pallas_call x11, Pallas kernels, called(): pl.pallas_call(kernel, out_shape=out_shape, in_specs=[whole] * 5 + [unrea...  21.5 us
    pallas_call x1, Pallas kernels, body(): pl.pallas_call(local_kernel, out_shape=(small, large, jax.ShapeDtypeStruc...  20.4 us
    ppermute x9, starting transfers between devices, exchanged(): lax.ppermute(array, 'tm', [(i, i ^ 2 ** level) for i in range(devices)])  10.6 us
    ppermute x9, waiting for transfers between devices, exchanged(): lax.ppermute(array, 'tm', [(i, i ^ 2 ** level) for i in range(devices)])  10.4 us
    pallas_call x1, Pallas kernels, body(): pl.pallas_call(functools.partial(final_kernel, levels, steps), out_shape=...  5.2 us
  transfers between devices with their start and end apart: 9, of which 6 were waited for; matrix products, arithmetic and copies ran while one was open for 0% of the time, Pallas kernels for 22%

profile of v1, /device:TPU:0, one launch (start us, length us, event | category | flops | bytes accessed | tf_op | source)
XLA Modules:
  0.0 69.0 jit_solution(8039659331927205426)
XLA Ops:
  0.0 20.4 %local.1 = (f32[136,128]{1,0:T(8,128)}, f32[264,128]{1,0:T(8,128)}, f32[7,264,128]{2,1,0:T(8,128)}) custom-call(f32[8,128,128]{2,1,0:T(8,128)} %trans_hbm.1, f32[8,128]{1,0:T(8,128)} %prec_hbm.1, f32[8,128]{1,0:T(8,128)} %obs_hbm.1), custom_call_target="tpu_custom_call" | custom-call | tf_op jit(solution)/shard_map/local/pallas_call | solution.py:314
  20.4 0.5 collective-permute-start
  20.9 0.0 copy-start.1
  20.9 0.1 collective-permute-start.1
  21.0 1.0 %collective-permute-done.came_near_ref.refs_2_ = f32[136,128]{1,0:T(8,128)S(1)} collective-permute-done((f32[136,128]{1,0:T(8,128)}, f32[136,128]{1,0:T(8,128)S(1)}, u32[]{:S(2)}, u32[]{:S(2)}) %collective-permute-start) | collective-permute-done | bytes 69664 | tf_op jit(solution)/shard_map/ppermute | solution.py:334
  22.1 0.0 copy-start.2
  22.1 0.9 %copy-done.2 = f32[136,128]{1,0:T(8,128)S(1)} copy-done((f32[136,128]{1,0:T(8,128)S(1)}, f32[136,128]{1,0:T(8,128)}, u32[]{:S(2)}) %copy-start.2) | copy-done | bytes 69656
  22.9 2.9 %inverse.4.inv_ref.refs_0_ = f32[128,128]{1,0:T(8,128)S(1)} custom-call(f32[136,128]{1,0:T(8,128)S(1)} %copy-done.2, f32[136,128]{1,0:T(8,128)S(1)} %collective-permute-done.came_near_ref.refs_2_), custom_call_target="tpu_custom_call" | custom-call | flops 6291456000 | bytes 196608 | tf_op jit(solution)/shard_map/inverse/pallas_call | solution.py:339
  25.9 0.0 collective-permute-done.1.came_far_ref.refs_4_
  25.9 0.0 copy-done.1
  25.9 0.6 near.3.near_ref.refs_5_.refs_1_
  26.5 2.9 %collective-permute-start.2 = (f32[136,128]{1,0:T(8,128)S(1)}, f32[136,128]{1,0:T(8,128)S(1)}, u32[]{:S(2)}, u32[]{:S(2)}) collective-permute-start(f32[136,128]{1,0:T(8,128)S(1)} %near.3.near_ref.refs_5_.refs_1_), channel_id=1, source_target_pairs={{0,2},{1,3},{2,0},{3,1},{4,6},{5,7},{6,4},{7,5},{8,10},{9,11},{10,... | collective-permute-start | bytes 208904 | tf_op jit(solution)/shard_map/ppermute | solution.py:334
  29.4 1.0 %far.3 = (f32[264,128]{1,0:T(8,128)S(1)}, f32[264,128]{1,0:T(8,128)S(1)}) custom-call(f32[128,128]{1,0:T(8,128)S(1)} %inverse.4.inv_ref.refs_0_, f32[136,128]{1,0:T(8,128)S(1)} %copy-done.2, f32[136,128]{1,0:T(8,128)S(1)} %collective-permute-done.came_near_ref.refs_2_, f32[264,128]{1,0:T(8,128)S(1)} %copy-done.1, ...), custom_call_target="tpu_custom_call" | custom-call | flops 1468006400 | bytes 196608 | tf_op jit(solution)/shard_map/far/pallas_call | solution.py:339
  30.5 0.1 collective-permute-start.3
  30.5 1.4 %collective-permute-done.2.came_near_ref.refs_2_ = f32[136,128]{1,0:T(8,128)S(1)} collective-permute-done((f32[136,128]{1,0:T(8,128)S(1)}, f32[136,128]{1,0:T(8,128)S(1)}, u32[]{:S(2)}, u32[]{:S(2)}) %collective-permute-start.2) | collective-permute-done | bytes 69664 | tf_op jit(solution)/shard_map/ppermute | solution.py:334
  31.9 2.9 %inverse.5.inv_ref.refs_0_ = f32[128,128]{1,0:T(8,128)S(1)} custom-call(f32[136,128]{1,0:T(8,128)S(1)} %near.3.near_ref.refs_5_.refs_1_, f32[136,128]{1,0:T(8,128)S(1)} %collective-permute-done.2.came_near_ref.refs_2_), custom_call_target="tpu_custom_call" | custom-call | flops 6291456000 | bytes 196608 | tf_op jit(solution)/shard_map/inverse/pallas_call | solution.py:339
  34.9 1.0 %collective-permute-done.3.came_far_ref.refs_4_ = f32[264,128]{1,0:T(8,128)S(1)} collective-permute-done((f32[264,128]{1,0:T(8,128)S(1)}, f32[264,128]{1,0:T(8,128)S(1)}, u32[]{:S(2)}, u32[]{:S(2)}) %collective-permute-start.3) | collective-permute-done | bytes 135200 | tf_op jit(solution)/shard_map/ppermute | solution.py:334
  35.9 0.6 near.4.near_ref.refs_5_.refs_1_
  36.5 1.6 %collective-permute-start.4 = (f32[136,128]{1,0:T(8,128)S(1)}, f32[136,128]{1,0:T(8,128)S(1)}, u32[]{:S(2)}, u32[]{:S(2)}) collective-permute-start(f32[136,128]{1,0:T(8,128)S(1)} %near.4.near_ref.refs_5_.refs_1_), channel_id=1, source_target_pairs={{0,4},{1,5},{2,6},{3,7},{4,0},{5,1},{6,2},{7,3},{8,12},{9,13},{10,... | collective-permute-start | bytes 208904 | tf_op jit(solution)/shard_map/ppermute | solution.py:334
  38.1 1.0 %far.4 = (f32[264,128]{1,0:T(8,128)S(1)}, f32[264,128]{1,0:T(8,128)S(1)}) custom-call(f32[128,128]{1,0:T(8,128)S(1)} %inverse.5.inv_ref.refs_0_, f32[136,128]{1,0:T(8,128)S(1)} %near.3.near_ref.refs_5_.refs_1_, f32[136,128]{1,0:T(8,128)S(1)} %collective-permute-done.2.came_near_ref.refs_2_, f32[264,128]{1,0:T(8,128)S(1)} %get-tuple-element.19.far_ref.refs_3_, ...), custom_call_target="tpu_custom_call" | custom-call | flops 1468006400 | bytes 196608 | tf_op jit(solution)/shard_map/far/pallas_call | solution.py:339
  39.2 0.6 collective-permute-start.5
  39.7 1.7 %collective-permute-done.4.came_near_ref.refs_2_ = f32[136,128]{1,0:T(8,128)S(1)} collective-permute-done((f32[136,128]{1,0:T(8,128)S(1)}, f32[136,128]{1,0:T(8,128)S(1)}, u32[]{:S(2)}, u32[]{:S(2)}) %collective-permute-start.4) | collective-permute-done | bytes 69664 | tf_op jit(solution)/shard_map/ppermute | solution.py:334
  41.4 2.9 %inverse.6.inv_ref.refs_0_ = f32[128,128]{1,0:T(8,128)S(1)} custom-call(f32[136,128]{1,0:T(8,128)S(1)} %near.4.near_ref.refs_5_.refs_1_, f32[136,128]{1,0:T(8,128)S(1)} %collective-permute-done.4.came_near_ref.refs_2_), custom_call_target="tpu_custom_call" | custom-call | flops 6291456000 | bytes 196608 | tf_op jit(solution)/shard_map/inverse/pallas_call | solution.py:339
  44.3 0.0 collective-permute-done.5.came_far_ref.refs_4_
  44.3 0.6 near.5.near_ref.refs_5_.refs_1_
  45.0 1.6 %collective-permute-start.6 = (f32[136,128]{1,0:T(8,128)S(1)}, f32[136,128]{1,0:T(8,128)S(1)}, u32[]{:S(2)}, u32[]{:S(2)}) collective-permute-start(f32[136,128]{1,0:T(8,128)S(1)} %near.5.near_ref.refs_5_.refs_1_), channel_id=1, source_target_pairs={{0,8},{1,9},{2,10},{3,11},{4,12},{5,13},{6,14},{7,15},{8,0},{9,1},... | collective-permute-start | bytes 208904 | tf_op jit(solution)/shard_map/ppermute | solution.py:334
  46.6 1.0 %far.5 = (f32[264,128]{1,0:T(8,128)S(1)}, f32[264,128]{1,0:T(8,128)S(1)}) custom-call(f32[128,128]{1,0:T(8,128)S(1)} %inverse.6.inv_ref.refs_0_, f32[136,128]{1,0:T(8,128)S(1)} %near.4.near_ref.refs_5_.refs_1_, f32[136,128]{1,0:T(8,128)S(1)} %collective-permute-done.4.came_near_ref.refs_2_, f32[264,128]{1,0:T(8,128)S(1)} %get-tuple-element.20.far_ref.refs_3_, ...), custom_call_target="tpu_custom_call" | custom-call | flops 1468006400 | bytes 196608 | tf_op jit(solution)/shard_map/far/pallas_call | solution.py:339
  47.6 0.5 collective-permute-start.7
  48.2 1.9 %collective-permute-done.6.came_near_ref.refs_2_ = f32[136,128]{1,0:T(8,128)S(1)} collective-permute-done((f32[136,128]{1,0:T(8,128)S(1)}, f32[136,128]{1,0:T(8,128)S(1)}, u32[]{:S(2)}, u32[]{:S(2)}) %collective-permute-start.6) | collective-permute-done | bytes 69664 | tf_op jit(solution)/shard_map/ppermute | solution.py:334
  50.1 3.2 %inverse.7.refs_0_ = f32[128,128]{1,0:T(8,128)S(1)} custom-call(f32[136,128]{1,0:T(8,128)S(1)} %near.5.near_ref.refs_5_.refs_1_, f32[136,128]{1,0:T(8,128)S(1)} %collective-permute-done.6.came_near_ref.refs_2_), custom_call_target="tpu_custom_call" | custom-call | flops 6291456000 | bytes 196608 | tf_op jit(solution)/shard_map/inverse/pallas_call | solution.py:339
  53.3 0.0 copy-start
  53.3 0.0 collective-permute-done.7.refs_4_
  53.3 4.5 %closing.1 = (f32[136,128]{1,0:T(8,128)S(1)}, f32[264,128]{1,0:T(8,128)S(1)}, f32[136,128]{1,0:T(8,128)S(1)}) custom-call(f32[128,128]{1,0:T(8,128)S(1)} %inverse.7.refs_0_, f32[136,128]{1,0:T(8,128)S(1)} %near.5.near_ref.refs_5_.refs_1_, f32[136,128]{1,0:T(8,128)S(1)} %collective-permute-done.6.came_near_ref.refs_2_, ...), custom_call_target="tpu_custom_call" | custom-call | flops 4194304000 | bytes 196608 | tf_op jit(solution)/shard_map/closing/pallas_call | solution.py:339
  57.8 2.6 %collective-permute-start.8 = (f32[136,128]{1,0:T(8,128)S(1)}, f32[136,128]{1,0:T(8,128)S(1)}, u32[]{:S(2)}, u32[]{:S(2)}) collective-permute-start(f32[136,128]{1,0:T(8,128)S(1)} %get-tuple-element.22.refs_0_), channel_id=1, source_target_pairs={{0,16},{1,17},{2,18},{3,19},{4,20},{5,21},{6,22},{7,23},{8,24},{9,... | collective-permute-start | bytes 208904 | tf_op jit(solution)/shard_map/ppermute | solution.py:334
  60.5 3.4 %collective-permute-done.8.refs_1_ = f32[136,128]{1,0:T(8,128)S(1)} collective-permute-done((f32[136,128]{1,0:T(8,128)S(1)}, f32[136,128]{1,0:T(8,128)S(1)}, u32[]{:S(2)}, u32[]{:S(2)}) %collective-permute-start.8) | collective-permute-done | bytes 69664 | tf_op jit(solution)/shard_map/ppermute | solution.py:334
  63.8 0.0 copy-done
  63.8 5.2 %final.1 = f32[8,128]{1,0:T(8,128)} custom-call(f32[136,128]{1,0:T(8,128)S(1)} %get-tuple-element.22.refs_0_, f32[136,128]{1,0:T(8,128)S(1)} %collective-permute-done.8.refs_1_, f32[264,128]{1,0:T(8,128)S(1)} %get-tuple-element.23.refs_2_, f32[264,128]{1,0:T(8,128)S(1)} %get-tuple-element.24.refs_3_, f32[264,128]{1,0:T(8,128)S(1)} %get-tuple-element.25.refs_4_, ...), custom_call_target="tpu_custom_call" | custom-call | tf_op jit(solution)/shard_map/final/pallas_call | solution.py:367
Async XLA Ops:
  20.4 1.6 %collective-permute-start = (f32[136,128]{1,0:T(8,128)}, f32[136,128]{1,0:T(8,128)S(1)}, u32[]{:S(2)}, u32[]{:S(2)}) collective-permute-start(f32[136,128]{1,0:T(8,128)} %get-tuple-element.17.near_ref.refs_1_), channel_id=1, source_target_pairs={{0,1},{1,0},{2,3},{3,2},{4,5},{5,4},{6,7},{7,6},{8,9},{9,8},{10,11... | collective-permute-start | bytes 208904 | tf_op jit(solution)/shard_map/ppermute | solution.py:334
  20.9 5.0 %copy-start.1 = (f32[264,128]{1,0:T(8,128)S(1)}, f32[264,128]{1,0:T(8,128)}, u32[]{:S(2)}) copy-start(f32[264,128]{1,0:T(8,128)} %get-tuple-element.18.far_ref.refs_3_) | copy-start | bytes 405508
  20.9 4.9 %collective-permute-start.1 = (f32[264,128]{1,0:T(8,128)}, f32[264,128]{1,0:T(8,128)S(1)}, u32[]{:S(2)}, u32[]{:S(2)}) collective-permute-start(f32[264,128]{1,0:T(8,128)} %get-tuple-element.18.far_ref.refs_3_), channel_id=1, source_target_pairs={{0,1},{1,0},{2,3},{3,2},{4,5},{5,4},{6,7},{7,6},{8,9},{9,8},{10,11... | collective-permute-start | bytes 405512 | tf_op jit(solution)/shard_map/ppermute | solution.py:334
  22.1 0.9 %copy-start.2 = (f32[136,128]{1,0:T(8,128)S(1)}, f32[136,128]{1,0:T(8,128)}, u32[]{:S(2)}) copy-start(f32[136,128]{1,0:T(8,128)} %get-tuple-element.17.near_ref.refs_1_) | copy-start | bytes 208900
  26.5 5.4 %collective-permute-start.2 = (f32[136,128]{1,0:T(8,128)S(1)}, f32[136,128]{1,0:T(8,128)S(1)}, u32[]{:S(2)}, u32[]{:S(2)}) collective-permute-start(f32[136,128]{1,0:T(8,128)S(1)} %near.3.near_ref.refs_5_.refs_1_), channel_id=1, source_target_pairs={{0,2},{1,3},{2,0},{3,1},{4,6},{5,7},{6,4},{7,5},{8,10},{9,11},{10,... | collective-permute-start | bytes 208904 | tf_op jit(solution)/shard_map/ppermute | solution.py:334
  30.5 5.4 %collective-permute-start.3 = (f32[264,128]{1,0:T(8,128)S(1)}, f32[264,128]{1,0:T(8,128)S(1)}, u32[]{:S(2)}, u32[]{:S(2)}) collective-permute-start(f32[264,128]{1,0:T(8,128)S(1)} %get-tuple-element.19.far_ref.refs_3_), channel_id=1, source_target_pairs={{0,2},{1,3},{2,0},{3,1},{4,6},{5,7},{6,4},{7,5},{8,10},{9,11},{10,... | collective-permute-start | bytes 405512 | tf_op jit(solution)/shard_map/ppermute | solution.py:334
  36.5 4.8 %collective-permute-start.4 = (f32[136,128]{1,0:T(8,128)S(1)}, f32[136,128]{1,0:T(8,128)S(1)}, u32[]{:S(2)}, u32[]{:S(2)}) collective-permute-start(f32[136,128]{1,0:T(8,128)S(1)} %near.4.near_ref.refs_5_.refs_1_), channel_id=1, source_target_pairs={{0,4},{1,5},{2,6},{3,7},{4,0},{5,1},{6,2},{7,3},{8,12},{9,13},{10,... | collective-permute-start | bytes 208904 | tf_op jit(solution)/shard_map/ppermute | solution.py:334
  39.2 5.2 %collective-permute-start.5 = (f32[264,128]{1,0:T(8,128)S(1)}, f32[264,128]{1,0:T(8,128)S(1)}, u32[]{:S(2)}, u32[]{:S(2)}) collective-permute-start(f32[264,128]{1,0:T(8,128)S(1)} %get-tuple-element.20.far_ref.refs_3_), channel_id=1, source_target_pairs={{0,4},{1,5},{2,6},{3,7},{4,0},{5,1},{6,2},{7,3},{8,12},{9,13},{10,... | collective-permute-start | bytes 405512 | tf_op jit(solution)/shard_map/ppermute | solution.py:334
  45.0 5.1 %collective-permute-start.6 = (f32[136,128]{1,0:T(8,128)S(1)}, f32[136,128]{1,0:T(8,128)S(1)}, u32[]{:S(2)}, u32[]{:S(2)}) collective-permute-start(f32[136,128]{1,0:T(8,128)S(1)} %near.5.near_ref.refs_5_.refs_1_), channel_id=1, source_target_pairs={{0,8},{1,9},{2,10},{3,11},{4,12},{5,13},{6,14},{7,15},{8,0},{9,1},... | collective-permute-start | bytes 208904 | tf_op jit(solution)/shard_map/ppermute | solution.py:334
  47.6 5.6 %collective-permute-start.7 = (f32[264,128]{1,0:T(8,128)S(1)}, f32[264,128]{1,0:T(8,128)S(1)}, u32[]{:S(2)}, u32[]{:S(2)}) collective-permute-start(f32[264,128]{1,0:T(8,128)S(1)} %get-tuple-element.21.refs_3_), channel_id=1, source_target_pairs={{0,8},{1,9},{2,10},{3,11},{4,12},{5,13},{6,14},{7,15},{8,0},{9,1},... | collective-permute-start | bytes 405512 | tf_op jit(solution)/shard_map/ppermute | solution.py:334
  53.3 10.6 %copy-start = (f32[7,264,128]{2,1,0:T(8,128)S(1)}, f32[7,264,128]{2,1,0:T(8,128)}, u32[]{:S(2)}) copy-start(f32[7,264,128]{2,1,0:T(8,128)} %get-tuple-element.28.refs_7_) | copy-start | bytes 2838532
  57.8 6.0 %collective-permute-start.8 = (f32[136,128]{1,0:T(8,128)S(1)}, f32[136,128]{1,0:T(8,128)S(1)}, u32[]{:S(2)}, u32[]{:S(2)}) collective-permute-start(f32[136,128]{1,0:T(8,128)S(1)} %get-tuple-element.22.refs_0_), channel_id=1, source_target_pairs={{0,16},{1,17},{2,18},{3,19},{4,20},{5,21},{6,22},{7,23},{8,24},{9,... | collective-permute-start | bytes 208904 | tf_op jit(solution)/shard_map/ppermute | solution.py:334

commit v2 on v1

--- a/solution.py
+++ b/solution.py
@@ -233,41 +233,50 @@
     near_out[n : n + ROWS] = jnp.where(next_left, v, u) + gram[n : n + ROWS]
 
 
-def merged(level, inv_ref, near_ref, came_near_ref, far_ref, came_far_ref):
+def far_kernel(level, *refs):
+    inv_ref, near_ref, came_near_ref, far_ref, came_far_ref, _, far_out, z_ref = refs
     n = near_ref.shape[1]
     alpha, gamma, beta_low, beta_high, u, v = parts(level, far_ref, came_far_ref)
     target = near_ref[n : n + ROWS] + came_near_ref[n : n + ROWS]
-    z, gram = eliminated(inv_ref[...], jnp.concatenate([beta_low, beta_high, target], axis=0))
-    return (
-        z,
-        alpha - gram[0:n, 0:n],
-        gamma - gram[n : 2 * n, n : 2 * n],
-        gram[0:n, n : 2 * n],
-        gram[n : 2 * n, 0:n],
-        u[0:1] + gram[2 * n : 2 * n + 1, 0:n],
-        v[0:1] + gram[2 * n : 2 * n + 1, n : 2 * n],
-    )
-
-
-def far_kernel(level, *refs):
-    far_out, z_ref = refs[6:]
-    z, alpha, gamma, beta_t, beta, u, v = merged(level, *refs[:5])
+    z = dot(jnp.concatenate([beta_low, beta_high, target], axis=0), inv_ref[...])
     z_ref[...] = z
-    write_far(bit_of("tm", level + 1) == 0, far_out, alpha, gamma, beta_t, beta, u, v)
+    next_left = bit_of("tm", level + 1) == 0
+    own = jnp.where(next_left, beta_low, beta_high)
+    other = jnp.where(next_left, beta_high, beta_low)
+    z_own = jnp.where(next_left, z[0:n], z[n : 2 * n])
+    gram = dot(
+        jnp.concatenate([z_own, z[2 * n : 2 * n + ROWS]], axis=0),
+        jnp.concatenate([own, other], axis=0),
+        ((1,), (1,)),
+    )
+    far_out[0:n] = jnp.where(next_left, alpha, gamma) - gram[0:n, 0:n]
+    far_out[n : 2 * n] = gram[0:n, n : 2 * n]
+    far_out[2 * n : 2 * n + ROWS] = jnp.where(next_left, u, v) + gram[n : n + ROWS, 0:n]
 
 
 def closing_kernel(level, *refs):
-    small_ref, z_ref, first_ref = refs[5:]
-    z, alpha, gamma, _, beta, u, v = merged(level, *refs[:5])
-    n = alpha.shape[0]
-    z_ref[...] = z
+    inv_ref, near_ref, came_near_ref, far_ref, came_far_ref, small_ref, z_ref, first_ref = refs
+    n = near_ref.shape[1]
+    alpha, gamma, beta_low, beta_high, u, v = parts(level, far_ref, came_far_ref)
+    target = near_ref[n : n + ROWS] + came_near_ref[n : n + ROWS]
+    z_low = dot(jnp.concatenate([beta_low, target], axis=0), inv_ref[...])
+    gram = dot(z_low, beta_low, ((1,), (1,)))
+    alpha = alpha - gram[0:n]
+    u = u + gram[n : n + ROWS]
     (inverse,) = inverses([alpha], True)
-    first = dot(jnp.concatenate([beta, padded(u)], axis=0), inverse)
+    z_high = dot(beta_high, inv_ref[...])
+    z_ref[0:n] = z_low[0:n]
+    z_ref[n : 2 * n] = z_high
+    z_ref[2 * n : 2 * n + ROWS] = z_low[n : n + ROWS]
+    gamma = gamma - dot(z_high, beta_high, ((1,), (1,)))
+    beta = dot(z_high, beta_low, ((1,), (1,)))
+    v = v + dot(z_low[n : n + ROWS], beta_high, ((1,), (1,)))
+    first = dot(jnp.concatenate([beta, u], axis=0), inverse)
     first_ref[...] = first
     gram = dot(first, beta, ((1,), (1,)))
     is_lower = bit_of("tm", level + 1) == 0
     small_ref[0:n] = jnp.where(is_lower, gamma - gram[0:n], alpha)
-    small_ref[n : n + ROWS] = padded(jnp.where(is_lower, v + gram[n : n + 1], u))
+    small_ref[n : n + ROWS] = jnp.where(is_lower, v + gram[n : n + ROWS], u)
 
 
 def between(z, low, high):
@@ -303,15 +312,10 @@
     out_ref[...] = jnp.concatenate([states[t] for t in range(steps)], axis=0)
 
 
-def body(transition, obs_precision, observations):
-    steps, n = obs_precision.shape
-    devices = lax.axis_size("tm")
-    levels = devices.bit_length() - 1
-    params = pltpu.CompilerParams(vmem_limit_bytes=48 * 2**20)
+def local_call(steps, n, name):
     small = jax.ShapeDtypeStruct((n + ROWS, n), jnp.float32)
     large = jax.ShapeDtypeStruct((2 * n + ROWS, n), jnp.float32)
-    square = jax.ShapeDtypeStruct((n, n), jnp.float32)
-    near, far, local_z = pl.pallas_call(
+    return pl.pallas_call(
         local_kernel,
         out_shape=(small, large, jax.ShapeDtypeStruct((steps - 1,) + large.shape, jnp.float32)),
         in_specs=[pl.BlockSpec(memory_space=pltpu.HBM)] * 3,
@@ -326,8 +330,19 @@
             pltpu.SemaphoreType.DMA((3,)),
         ],
         compiler_params=pltpu.CompilerParams(vmem_limit_bytes=60 * 2**20),
-        name="local",
-    )(transition, obs_precision, observations)
+        name=name,
+    )
+
+
+def body(transition, obs_precision, observations):
+    steps, n = obs_precision.shape
+    devices = lax.axis_size("tm")
+    levels = devices.bit_length() - 1
+    params = pltpu.CompilerParams(vmem_limit_bytes=48 * 2**20)
+    small = jax.ShapeDtypeStruct((n + ROWS, n), jnp.float32)
+    large = jax.ShapeDtypeStruct((2 * n + ROWS, n), jnp.float32)
+    square = jax.ShapeDtypeStruct((n, n), jnp.float32)
+    near, far, local_z = local_call(steps, n, "local")(transition, obs_precision, observations)
     zs = []
 
     def exchanged(array, level):

time: 69.2 us -> 67.7 us (0.978)
  Pallas kernels: 47.1 us -> 46.1 us
    pallas_call x11, Pallas kernels: 21.5 us -> 20.5 us  [called(): pl.pallas_call(kernel, out_shape=out_shape, in_specs=[whole] * 5 + [unrea...]
  transfers between devices with their start and end apart: 9 -> 9, of which waited for: 6 -> 6; matrix products, arithmetic and copies ran while one was open for 0% -> 0% of each run, Pallas kernels for 22% -> 21%
where the time goes in v2:
time: 67.7 us; the launch traced here: 67.5 us
  Pallas kernels  46.1 us (68%)
  starting transfers between devices  10.5 us (16%)
  waiting for transfers between devices  9.9 us (15%)
  local copies, waits for them, and re-layouts  0.89 us (1%)
    pallas_call x11, Pallas kernels, called(): pl.pallas_call(kernel, out_shape=out_shape, in_specs=[whole] * 5 + [unrea...  20.5 us
    pallas_call x1, Pallas kernels, body(): local_call(steps, n, 'local')(transition, obs_precision, observations)  20.4 us
    ppermute x9, starting transfers between devices, exchanged(): lax.ppermute(array, 'tm', [(i, i ^ 2 ** level) for i in range(devices)])  10.5 us
    ppermute x9, waiting for transfers between devices, exchanged(): lax.ppermute(array, 'tm', [(i, i ^ 2 ** level) for i in range(devices)])  9.9 us
    pallas_call x1, Pallas kernels, body(): pl.pallas_call(functools.partial(final_kernel, levels, steps), out_shape=...  5.2 us
  transfers between devices with their start and end apart: 9, of which 6 were waited for; matrix products, arithmetic and copies ran while one was open for 0% of the time, Pallas kernels for 21%

profile of v2, /device:TPU:0, one launch (start us, length us, event | category | flops | bytes accessed | tf_op | source)
XLA Modules:
  0.0 67.5 jit_solution(2375653902337892805)
XLA Ops:
  0.0 20.4 %local.1 = (f32[136,128]{1,0:T(8,128)}, f32[264,128]{1,0:T(8,128)}, f32[7,264,128]{2,1,0:T(8,128)}) custom-call(f32[8,128,128]{2,1,0:T(8,128)} %trans_hbm.1, f32[8,128]{1,0:T(8,128)} %prec_hbm.1, f32[8,128]{1,0:T(8,128)} %obs_hbm.1), custom_call_target="tpu_custom_call" | custom-call | tf_op jit(solution)/shard_map/local/pallas_call | solution.py:345
  20.4 0.5 collective-permute-start
  20.9 0.0 copy-start.1
  20.9 0.1 collective-permute-start.1
  21.0 1.0 %collective-permute-done.came_near_ref.refs_2_ = f32[136,128]{1,0:T(8,128)S(1)} collective-permute-done((f32[136,128]{1,0:T(8,128)}, f32[136,128]{1,0:T(8,128)S(1)}, u32[]{:S(2)}, u32[]{:S(2)}) %collective-permute-start) | collective-permute-done | bytes 69664 | tf_op jit(solution)/shard_map/ppermute | solution.py:349
  22.1 0.0 copy-start.2
  22.1 0.9 %copy-done.2 = f32[136,128]{1,0:T(8,128)S(1)} copy-done((f32[136,128]{1,0:T(8,128)S(1)}, f32[136,128]{1,0:T(8,128)}, u32[]{:S(2)}) %copy-start.2) | copy-done | bytes 69656
  22.9 2.9 %inverse.4.inv_ref.refs_0_ = f32[128,128]{1,0:T(8,128)S(1)} custom-call(f32[136,128]{1,0:T(8,128)S(1)} %copy-done.2, f32[136,128]{1,0:T(8,128)S(1)} %collective-permute-done.came_near_ref.refs_2_), custom_call_target="tpu_custom_call" | custom-call | flops 6291456000 | bytes 196608 | tf_op jit(solution)/shard_map/inverse/pallas_call | solution.py:354
  25.9 0.0 collective-permute-done.1.came_far_ref.refs_4_
  25.9 0.0 copy-done.1
  25.9 0.6 near.3.near_ref.refs_5_.refs_1_
  26.5 2.9 %collective-permute-start.2 = (f32[136,128]{1,0:T(8,128)S(1)}, f32[136,128]{1,0:T(8,128)S(1)}, u32[]{:S(2)}, u32[]{:S(2)}) collective-permute-start(f32[136,128]{1,0:T(8,128)S(1)} %near.3.near_ref.refs_5_.refs_1_), channel_id=1, source_target_pairs={{0,2},{1,3},{2,0},{3,1},{4,6},{5,7},{6,4},{7,5},{8,10},{9,11},{10,... | collective-permute-start | bytes 208904 | tf_op jit(solution)/shard_map/ppermute | solution.py:349
  29.4 0.8 %far.3 = (f32[264,128]{1,0:T(8,128)S(1)}, f32[264,128]{1,0:T(8,128)S(1)}) custom-call(f32[128,128]{1,0:T(8,128)S(1)} %inverse.4.inv_ref.refs_0_, f32[136,128]{1,0:T(8,128)S(1)} %copy-done.2, f32[136,128]{1,0:T(8,128)S(1)} %collective-permute-done.came_near_ref.refs_2_, f32[264,128]{1,0:T(8,128)S(1)} %copy-done.1, ...), custom_call_target="tpu_custom_call" | custom-call | flops 1468006400 | bytes 196608 | tf_op jit(solution)/shard_map/far/pallas_call | solution.py:354
  30.2 0.1 collective-permute-start.3
  30.3 1.7 %collective-permute-done.2.came_near_ref.refs_2_ = f32[136,128]{1,0:T(8,128)S(1)} collective-permute-done((f32[136,128]{1,0:T(8,128)S(1)}, f32[136,128]{1,0:T(8,128)S(1)}, u32[]{:S(2)}, u32[]{:S(2)}) %collective-permute-start.2) | collective-permute-done | bytes 69664 | tf_op jit(solution)/shard_map/ppermute | solution.py:349
  32.0 2.9 %inverse.5.inv_ref.refs_0_ = f32[128,128]{1,0:T(8,128)S(1)} custom-call(f32[136,128]{1,0:T(8,128)S(1)} %near.3.near_ref.refs_5_.refs_1_, f32[136,128]{1,0:T(8,128)S(1)} %collective-permute-done.2.came_near_ref.refs_2_), custom_call_target="tpu_custom_call" | custom-call | flops 6291456000 | bytes 196608 | tf_op jit(solution)/shard_map/inverse/pallas_call | solution.py:354
  34.9 0.8 %collective-permute-done.3.came_far_ref.refs_4_ = f32[264,128]{1,0:T(8,128)S(1)} collective-permute-done((f32[264,128]{1,0:T(8,128)S(1)}, f32[264,128]{1,0:T(8,128)S(1)}, u32[]{:S(2)}, u32[]{:S(2)}) %collective-permute-start.3) | collective-permute-done | bytes 135200 | tf_op jit(solution)/shard_map/ppermute | solution.py:349
  35.7 0.6 near.4.near_ref.refs_5_.refs_1_
  36.3 1.6 %collective-permute-start.4 = (f32[136,128]{1,0:T(8,128)S(1)}, f32[136,128]{1,0:T(8,128)S(1)}, u32[]{:S(2)}, u32[]{:S(2)}) collective-permute-start(f32[136,128]{1,0:T(8,128)S(1)} %near.4.near_ref.refs_5_.refs_1_), channel_id=1, source_target_pairs={{0,4},{1,5},{2,6},{3,7},{4,0},{5,1},{6,2},{7,3},{8,12},{9,13},{10,... | collective-permute-start | bytes 208904 | tf_op jit(solution)/shard_map/ppermute | solution.py:349
  37.9 0.8 %far.4 = (f32[264,128]{1,0:T(8,128)S(1)}, f32[264,128]{1,0:T(8,128)S(1)}) custom-call(f32[128,128]{1,0:T(8,128)S(1)} %inverse.5.inv_ref.refs_0_, f32[136,128]{1,0:T(8,128)S(1)} %near.3.near_ref.refs_5_.refs_1_, f32[136,128]{1,0:T(8,128)S(1)} %collective-permute-done.2.came_near_ref.refs_2_, f32[264,128]{1,0:T(8,128)S(1)} %get-tuple-element.19.far_ref.refs_3_, ...), custom_call_target="tpu_custom_call" | custom-call | flops 1468006400 | bytes 196608 | tf_op jit(solution)/shard_map/far/pallas_call | solution.py:354
  38.7 0.6 collective-permute-start.5
  39.2 2.1 %collective-permute-done.4.came_near_ref.refs_2_ = f32[136,128]{1,0:T(8,128)S(1)} collective-permute-done((f32[136,128]{1,0:T(8,128)S(1)}, f32[136,128]{1,0:T(8,128)S(1)}, u32[]{:S(2)}, u32[]{:S(2)}) %collective-permute-start.4) | collective-permute-done | bytes 69664 | tf_op jit(solution)/shard_map/ppermute | solution.py:349
  41.3 2.9 %inverse.6.inv_ref.refs_0_ = f32[128,128]{1,0:T(8,128)S(1)} custom-call(f32[136,128]{1,0:T(8,128)S(1)} %near.4.near_ref.refs_5_.refs_1_, f32[136,128]{1,0:T(8,128)S(1)} %collective-permute-done.4.came_near_ref.refs_2_), custom_call_target="tpu_custom_call" | custom-call | flops 6291456000 | bytes 196608 | tf_op jit(solution)/shard_map/inverse/pallas_call | solution.py:354
  44.2 0.0 collective-permute-done.5.came_far_ref.refs_4_
  44.3 0.6 near.5.near_ref.refs_5_.refs_1_
  44.9 1.6 %collective-permute-start.6 = (f32[136,128]{1,0:T(8,128)S(1)}, f32[136,128]{1,0:T(8,128)S(1)}, u32[]{:S(2)}, u32[]{:S(2)}) collective-permute-start(f32[136,128]{1,0:T(8,128)S(1)} %near.5.near_ref.refs_5_.refs_1_), channel_id=1, source_target_pairs={{0,8},{1,9},{2,10},{3,11},{4,12},{5,13},{6,14},{7,15},{8,0},{9,1},... | collective-permute-start | bytes 208904 | tf_op jit(solution)/shard_map/ppermute | solution.py:349
  46.5 0.8 %far.5 = (f32[264,128]{1,0:T(8,128)S(1)}, f32[264,128]{1,0:T(8,128)S(1)}) custom-call(f32[128,128]{1,0:T(8,128)S(1)} %inverse.6.inv_ref.refs_0_, f32[136,128]{1,0:T(8,128)S(1)} %near.4.near_ref.refs_5_.refs_1_, f32[136,128]{1,0:T(8,128)S(1)} %collective-permute-done.4.came_near_ref.refs_2_, f32[264,128]{1,0:T(8,128)S(1)} %get-tuple-element.20.far_ref.refs_3_, ...), custom_call_target="tpu_custom_call" | custom-call | flops 1468006400 | bytes 196608 | tf_op jit(solution)/shard_map/far/pallas_call | solution.py:354
  47.3 0.5 collective-permute-start.7
  47.8 1.7 %collective-permute-done.6.came_near_ref.refs_2_ = f32[136,128]{1,0:T(8,128)S(1)} collective-permute-done((f32[136,128]{1,0:T(8,128)S(1)}, f32[136,128]{1,0:T(8,128)S(1)}, u32[]{:S(2)}, u32[]{:S(2)}) %collective-permute-start.6) | collective-permute-done | bytes 69664 | tf_op jit(solution)/shard_map/ppermute | solution.py:349
  49.6 3.2 %inverse.7.refs_0_ = f32[128,128]{1,0:T(8,128)S(1)} custom-call(f32[136,128]{1,0:T(8,128)S(1)} %near.5.near_ref.refs_5_.refs_1_, f32[136,128]{1,0:T(8,128)S(1)} %collective-permute-done.6.came_near_ref.refs_2_), custom_call_target="tpu_custom_call" | custom-call | flops 6291456000 | bytes 196608 | tf_op jit(solution)/shard_map/inverse/pallas_call | solution.py:354
  52.8 0.0 copy-start
  52.8 0.0 collective-permute-done.7.refs_4_
  52.8 4.3 %closing.1 = (f32[136,128]{1,0:T(8,128)S(1)}, f32[264,128]{1,0:T(8,128)S(1)}, f32[136,128]{1,0:T(8,128)S(1)}) custom-call(f32[128,128]{1,0:T(8,128)S(1)} %inverse.7.refs_0_, f32[136,128]{1,0:T(8,128)S(1)} %near.5.near_ref.refs_5_.refs_1_, f32[136,128]{1,0:T(8,128)S(1)} %collective-permute-done.6.came_near_ref.refs_2_, ...), custom_call_target="tpu_custom_call" | custom-call | flops 4194304000 | bytes 196608 | tf_op jit(solution)/shard_map/closing/pallas_call | solution.py:354
  57.1 2.6 %collective-permute-start.8 = (f32[136,128]{1,0:T(8,128)S(1)}, f32[136,128]{1,0:T(8,128)S(1)}, u32[]{:S(2)}, u32[]{:S(2)}) collective-permute-start(f32[136,128]{1,0:T(8,128)S(1)} %get-tuple-element.22.refs_0_), channel_id=1, source_target_pairs={{0,16},{1,17},{2,18},{3,19},{4,20},{5,21},{6,22},{7,23},{8,24},{9,... | collective-permute-start | bytes 208904 | tf_op jit(solution)/shard_map/ppermute | solution.py:349
  59.7 2.6 %collective-permute-done.8.refs_1_ = f32[136,128]{1,0:T(8,128)S(1)} collective-permute-done((f32[136,128]{1,0:T(8,128)S(1)}, f32[136,128]{1,0:T(8,128)S(1)}, u32[]{:S(2)}, u32[]{:S(2)}) %collective-permute-start.8) | collective-permute-done | bytes 69664 | tf_op jit(solution)/shard_map/ppermute | solution.py:349
  62.3 0.0 copy-done
  62.3 5.2 %final.1 = f32[8,128]{1,0:T(8,128)} custom-call(f32[136,128]{1,0:T(8,128)S(1)} %get-tuple-element.22.refs_0_, f32[136,128]{1,0:T(8,128)S(1)} %collective-permute-done.8.refs_1_, f32[264,128]{1,0:T(8,128)S(1)} %get-tuple-element.23.refs_2_, f32[264,128]{1,0:T(8,128)S(1)} %get-tuple-element.24.refs_3_, f32[264,128]{1,0:T(8,128)S(1)} %get-tuple-element.25.refs_4_, ...), custom_call_target="tpu_custom_call" | custom-call | tf_op jit(solution)/shard_map/final/pallas_call | solution.py:382
Async XLA Ops:
  20.4 1.6 %collective-permute-start = (f32[136,128]{1,0:T(8,128)}, f32[136,128]{1,0:T(8,128)S(1)}, u32[]{:S(2)}, u32[]{:S(2)}) collective-permute-start(f32[136,128]{1,0:T(8,128)} %get-tuple-element.17.near_ref.refs_1_), channel_id=1, source_target_pairs={{0,1},{1,0},{2,3},{3,2},{4,5},{5,4},{6,7},{7,6},{8,9},{9,8},{10,11... | collective-permute-start | bytes 208904 | tf_op jit(solution)/shard_map/ppermute | solution.py:349
  20.9 5.0 %copy-start.1 = (f32[264,128]{1,0:T(8,128)S(1)}, f32[264,128]{1,0:T(8,128)}, u32[]{:S(2)}) copy-start(f32[264,128]{1,0:T(8,128)} %get-tuple-element.18.far_ref.refs_3_) | copy-start | bytes 405508
  20.9 4.9 %collective-permute-start.1 = (f32[264,128]{1,0:T(8,128)}, f32[264,128]{1,0:T(8,128)S(1)}, u32[]{:S(2)}, u32[]{:S(2)}) collective-permute-start(f32[264,128]{1,0:T(8,128)} %get-tuple-element.18.far_ref.refs_3_), channel_id=1, source_target_pairs={{0,1},{1,0},{2,3},{3,2},{4,5},{5,4},{6,7},{7,6},{8,9},{9,8},{10,11... | collective-permute-start | bytes 405512 | tf_op jit(solution)/shard_map/ppermute | solution.py:349
  22.1 0.9 %copy-start.2 = (f32[136,128]{1,0:T(8,128)S(1)}, f32[136,128]{1,0:T(8,128)}, u32[]{:S(2)}) copy-start(f32[136,128]{1,0:T(8,128)} %get-tuple-element.17.near_ref.refs_1_) | copy-start | bytes 208900
  26.5 5.4 %collective-permute-start.2 = (f32[136,128]{1,0:T(8,128)S(1)}, f32[136,128]{1,0:T(8,128)S(1)}, u32[]{:S(2)}, u32[]{:S(2)}) collective-permute-start(f32[136,128]{1,0:T(8,128)S(1)} %near.3.near_ref.refs_5_.refs_1_), channel_id=1, source_target_pairs={{0,2},{1,3},{2,0},{3,1},{4,6},{5,7},{6,4},{7,5},{8,10},{9,11},{10,... | collective-permute-start | bytes 208904 | tf_op jit(solution)/shard_map/ppermute | solution.py:349
  30.2 5.4 %collective-permute-start.3 = (f32[264,128]{1,0:T(8,128)S(1)}, f32[264,128]{1,0:T(8,128)S(1)}, u32[]{:S(2)}, u32[]{:S(2)}) collective-permute-start(f32[264,128]{1,0:T(8,128)S(1)} %get-tuple-element.19.far_ref.refs_3_), channel_id=1, source_target_pairs={{0,2},{1,3},{2,0},{3,1},{4,6},{5,7},{6,4},{7,5},{8,10},{9,11},{10,... | collective-permute-start | bytes 405512 | tf_op jit(solution)/shard_map/ppermute | solution.py:349
  36.3 5.0 %collective-permute-start.4 = (f32[136,128]{1,0:T(8,128)S(1)}, f32[136,128]{1,0:T(8,128)S(1)}, u32[]{:S(2)}, u32[]{:S(2)}) collective-permute-start(f32[136,128]{1,0:T(8,128)S(1)} %near.4.near_ref.refs_5_.refs_1_), channel_id=1, source_target_pairs={{0,4},{1,5},{2,6},{3,7},{4,0},{5,1},{6,2},{7,3},{8,12},{9,13},{10,... | collective-permute-start | bytes 208904 | tf_op jit(solution)/shard_map/ppermute | solution.py:349
  38.7 5.6 %collective-permute-start.5 = (f32[264,128]{1,0:T(8,128)S(1)}, f32[264,128]{1,0:T(8,128)S(1)}, u32[]{:S(2)}, u32[]{:S(2)}) collective-permute-start(f32[264,128]{1,0:T(8,128)S(1)} %get-tuple-element.20.far_ref.refs_3_), channel_id=1, source_target_pairs={{0,4},{1,5},{2,6},{3,7},{4,0},{5,1},{6,2},{7,3},{8,12},{9,13},{10,... | collective-permute-start | bytes 405512 | tf_op jit(solution)/shard_map/ppermute | solution.py:349
  44.9 4.7 %collective-permute-start.6 = (f32[136,128]{1,0:T(8,128)S(1)}, f32[136,128]{1,0:T(8,128)S(1)}, u32[]{:S(2)}, u32[]{:S(2)}) collective-permute-start(f32[136,128]{1,0:T(8,128)S(1)} %near.5.near_ref.refs_5_.refs_1_), channel_id=1, source_target_pairs={{0,8},{1,9},{2,10},{3,11},{4,12},{5,13},{6,14},{7,15},{8,0},{9,1},... | collective-permute-start | bytes 208904 | tf_op jit(solution)/shard_map/ppermute | solution.py:349
  47.3 5.5 %collective-permute-start.7 = (f32[264,128]{1,0:T(8,128)S(1)}, f32[264,128]{1,0:T(8,128)S(1)}, u32[]{:S(2)}, u32[]{:S(2)}) collective-permute-start(f32[264,128]{1,0:T(8,128)S(1)} %get-tuple-element.21.refs_3_), channel_id=1, source_target_pairs={{0,8},{1,9},{2,10},{3,11},{4,12},{5,13},{6,14},{7,15},{8,0},{9,1},... | collective-permute-start | bytes 405512 | tf_op jit(solution)/shard_map/ppermute | solution.py:349
  52.8 9.6 %copy-start = (f32[7,264,128]{2,1,0:T(8,128)S(1)}, f32[7,264,128]{2,1,0:T(8,128)}, u32[]{:S(2)}) copy-start(f32[7,264,128]{2,1,0:T(8,128)} %get-tuple-element.28.refs_7_) | copy-start | bytes 2838532
  57.1 5.3 %collective-permute-start.8 = (f32[136,128]{1,0:T(8,128)S(1)}, f32[136,128]{1,0:T(8,128)S(1)}, u32[]{:S(2)}, u32[]{:S(2)}) collective-permute-start(f32[136,128]{1,0:T(8,128)S(1)} %get-tuple-element.22.refs_0_), channel_id=1, source_target_pairs={{0,16},{1,17},{2,18},{3,19},{4,20},{5,21},{6,22},{7,23},{8,24},{9,... | collective-permute-start | bytes 208904 | tf_op jit(solution)/shard_map/ppermute | solution.py:349

commit v3 on v2

--- a/solution.py
+++ b/solution.py
@@ -110,11 +110,6 @@
     return matrices
 
 
-def eliminated(inverse, sources):
-    z = dot(sources, inverse)
-    return z, dot(z, sources[: sources.shape[0] - ROWS], ((1,), (1,)))
-
-
 def padded(row):
     return jnp.concatenate([row, jnp.zeros((ROWS - 1, row.shape[1]), jnp.float32)], axis=0)
 
@@ -185,16 +180,33 @@
                 sources = jnp.concatenate(
                     [bwd_ref[low], fwd_ref[j], padded(vec_ref[j : j + 1])], axis=0
                 )
-                z, gram = eliminated(inv_ref[j], sources)
+                z = dot(sources, inv_ref[j])
                 z_ref[slot + k] = z
-                center_ref[low] = center_ref[low] - gram[0:n, 0:n]
-                center_ref[high] = center_ref[high] - gram[n : 2 * n, n : 2 * n]
-                vec_ref[low : low + 1] = vec_ref[low : low + 1] + gram[2 * n : 2 * n + 1, 0:n]
-                vec_ref[high : high + 1] = (
-                    vec_ref[high : high + 1] + gram[2 * n : 2 * n + 1, n : 2 * n]
-                )
-                fwd_ref[low] = gram[n : 2 * n, 0:n]
-                bwd_ref[low] = gram[0:n, n : 2 * n]
+                pair = sources[0 : 2 * n]
+                if len(odd) == 1:
+                    gram = dot(z, pair, ((1,), (1,)))
+                    low_part, high_part = gram[0:n, 0:n], gram[n : 2 * n, n : 2 * n]
+                    vec_part = gram[2 * n : 2 * n + 1]
+                    fwd_ref[low] = gram[n : 2 * n, 0:n]
+                    bwd_ref[low] = gram[0:n, n : 2 * n]
+                else:
+                    near_rows = z[0:n] if k % 2 == 0 else z[n : 2 * n]
+                    gram = dot(
+                        jnp.concatenate([near_rows, z[2 * n :]], axis=0), pair, ((1,), (1,))
+                    )
+                    vec_part = gram[n : n + 1]
+                    if k % 2 == 0:
+                        low_part = gram[0:n, 0:n]
+                        high_part = dot(z[n : 2 * n], pair[n:], ((1,), (1,)))
+                        bwd_ref[low] = gram[0:n, n : 2 * n]
+                    else:
+                        low_part = dot(z[0:n], pair[0:n], ((1,), (1,)))
+                        high_part = gram[0:n, n : 2 * n]
+                        fwd_ref[low] = gram[0:n, 0:n]
+                center_ref[low] = center_ref[low] - low_part
+                center_ref[high] = center_ref[high] - high_part
+                vec_ref[low : low + 1] = vec_ref[low : low + 1] + vec_part[:, 0:n]
+                vec_ref[high : high + 1] = vec_ref[high : high + 1] + vec_part[:, n : 2 * n]
 
         slot += len(odd)
         gap *= 2

time: 67.7 us -> 68 us (level)
  no operation moved by 1% of the time
where the time goes in v3:
time: 68 us; the launch traced here: 67.8 us
  Pallas kernels  46.3 us (68%)
  starting transfers between devices  10.6 us (16%)
  waiting for transfers between devices  9.89 us (15%)
  local copies, waits for them, and re-layouts  0.89 us (1%)
    pallas_call x1, Pallas kernels, body(): local_call(steps, n, 'local')(transition, obs_precision, observations)  20.6 us
    pallas_call x11, Pallas kernels, called(): pl.pallas_call(kernel, out_shape=out_shape, in_specs=[whole] * 5 + [unrea...  20.5 us
    ppermute x9, starting transfers between devices, exchanged(): lax.ppermute(array, 'tm', [(i, i ^ 2 ** level) for i in range(devices)])  10.6 us
    ppermute x9, waiting for transfers between devices, exchanged(): lax.ppermute(array, 'tm', [(i, i ^ 2 ** level) for i in range(devices)])  9.89 us
    pallas_call x1, Pallas kernels, body(): pl.pallas_call(functools.partial(final_kernel, levels, steps), out_shape=...  5.2 us
  transfers between devices with their start and end apart: 9, of which 6 were waited for; matrix products, arithmetic and copies ran while one was open for 0% of the time, Pallas kernels for 21%

profile of v3, /device:TPU:0, one launch (start us, length us, event | category | flops | bytes accessed | tf_op | source)
XLA Modules:
  0.0 67.8 jit_solution(10211680655336751859)
XLA Ops:
  0.0 20.6 %local.1 = (f32[136,128]{1,0:T(8,128)}, f32[264,128]{1,0:T(8,128)}, f32[7,264,128]{2,1,0:T(8,128)}) custom-call(f32[8,128,128]{2,1,0:T(8,128)} %trans_hbm.1, f32[8,128]{1,0:T(8,128)} %prec_hbm.1, f32[8,128]{1,0:T(8,128)} %obs_hbm.1), custom_call_target="tpu_custom_call" | custom-call | tf_op jit(solution)/shard_map/local/pallas_call | solution.py:357
  20.7 0.5 collective-permute-start
  21.2 0.0 copy-start.1
  21.2 0.1 collective-permute-start.1
  21.3 1.0 %collective-permute-done.came_near_ref.refs_2_ = f32[136,128]{1,0:T(8,128)S(1)} collective-permute-done((f32[136,128]{1,0:T(8,128)}, f32[136,128]{1,0:T(8,128)S(1)}, u32[]{:S(2)}, u32[]{:S(2)}) %collective-permute-start) | collective-permute-done | bytes 69664 | tf_op jit(solution)/shard_map/ppermute | solution.py:361
  22.3 0.0 copy-start.2
  22.3 0.9 %copy-done.2 = f32[136,128]{1,0:T(8,128)S(1)} copy-done((f32[136,128]{1,0:T(8,128)S(1)}, f32[136,128]{1,0:T(8,128)}, u32[]{:S(2)}) %copy-start.2) | copy-done | bytes 69656
  23.2 2.9 %inverse.4.inv_ref.refs_0_ = f32[128,128]{1,0:T(8,128)S(1)} custom-call(f32[136,128]{1,0:T(8,128)S(1)} %copy-done.2, f32[136,128]{1,0:T(8,128)S(1)} %collective-permute-done.came_near_ref.refs_2_), custom_call_target="tpu_custom_call" | custom-call | flops 6291456000 | bytes 196608 | tf_op jit(solution)/shard_map/inverse/pallas_call | solution.py:366
  26.1 0.0 collective-permute-done.1.came_far_ref.refs_4_
  26.1 0.0 copy-done.1
  26.1 0.6 near.3.near_ref.refs_5_.refs_1_
  26.8 2.9 %collective-permute-start.2 = (f32[136,128]{1,0:T(8,128)S(1)}, f32[136,128]{1,0:T(8,128)S(1)}, u32[]{:S(2)}, u32[]{:S(2)}) collective-permute-start(f32[136,128]{1,0:T(8,128)S(1)} %near.3.near_ref.refs_5_.refs_1_), channel_id=1, source_target_pairs={{0,2},{1,3},{2,0},{3,1},{4,6},{5,7},{6,4},{7,5},{8,10},{9,11},{10,... | collective-permute-start | bytes 208904 | tf_op jit(solution)/shard_map/ppermute | solution.py:361
  29.7 0.8 %far.3 = (f32[264,128]{1,0:T(8,128)S(1)}, f32[264,128]{1,0:T(8,128)S(1)}) custom-call(f32[128,128]{1,0:T(8,128)S(1)} %inverse.4.inv_ref.refs_0_, f32[136,128]{1,0:T(8,128)S(1)} %copy-done.2, f32[136,128]{1,0:T(8,128)S(1)} %collective-permute-done.came_near_ref.refs_2_, f32[264,128]{1,0:T(8,128)S(1)} %copy-done.1, ...), custom_call_target="tpu_custom_call" | custom-call | flops 1468006400 | bytes 196608 | tf_op jit(solution)/shard_map/far/pallas_call | solution.py:366
  30.5 0.1 collective-permute-start.3
  30.5 1.7 %collective-permute-done.2.came_near_ref.refs_2_ = f32[136,128]{1,0:T(8,128)S(1)} collective-permute-done((f32[136,128]{1,0:T(8,128)S(1)}, f32[136,128]{1,0:T(8,128)S(1)}, u32[]{:S(2)}, u32[]{:S(2)}) %collective-permute-start.2) | collective-permute-done | bytes 69664 | tf_op jit(solution)/shard_map/ppermute | solution.py:361
  32.2 2.9 %inverse.5.inv_ref.refs_0_ = f32[128,128]{1,0:T(8,128)S(1)} custom-call(f32[136,128]{1,0:T(8,128)S(1)} %near.3.near_ref.refs_5_.refs_1_, f32[136,128]{1,0:T(8,128)S(1)} %collective-permute-done.2.came_near_ref.refs_2_), custom_call_target="tpu_custom_call" | custom-call | flops 6291456000 | bytes 196608 | tf_op jit(solution)/shard_map/inverse/pallas_call | solution.py:366
  35.1 0.7 %collective-permute-done.3.came_far_ref.refs_4_ = f32[264,128]{1,0:T(8,128)S(1)} collective-permute-done((f32[264,128]{1,0:T(8,128)S(1)}, f32[264,128]{1,0:T(8,128)S(1)}, u32[]{:S(2)}, u32[]{:S(2)}) %collective-permute-start.3) | collective-permute-done | bytes 135200 | tf_op jit(solution)/shard_map/ppermute | solution.py:361
  35.9 0.6 near.4.near_ref.refs_5_.refs_1_
  36.5 1.6 %collective-permute-start.4 = (f32[136,128]{1,0:T(8,128)S(1)}, f32[136,128]{1,0:T(8,128)S(1)}, u32[]{:S(2)}, u32[]{:S(2)}) collective-permute-start(f32[136,128]{1,0:T(8,128)S(1)} %near.4.near_ref.refs_5_.refs_1_), channel_id=1, source_target_pairs={{0,4},{1,5},{2,6},{3,7},{4,0},{5,1},{6,2},{7,3},{8,12},{9,13},{10,... | collective-permute-start | bytes 208904 | tf_op jit(solution)/shard_map/ppermute | solution.py:361
  38.1 0.8 %far.4 = (f32[264,128]{1,0:T(8,128)S(1)}, f32[264,128]{1,0:T(8,128)S(1)}) custom-call(f32[128,128]{1,0:T(8,128)S(1)} %inverse.5.inv_ref.refs_0_, f32[136,128]{1,0:T(8,128)S(1)} %near.3.near_ref.refs_5_.refs_1_, f32[136,128]{1,0:T(8,128)S(1)} %collective-permute-done.2.came_near_ref.refs_2_, f32[264,128]{1,0:T(8,128)S(1)} %get-tuple-element.19.far_ref.refs_3_, ...), custom_call_target="tpu_custom_call" | custom-call | flops 1468006400 | bytes 196608 | tf_op jit(solution)/shard_map/far/pallas_call | solution.py:366
  38.9 0.6 collective-permute-start.5
  39.5 2.0 %collective-permute-done.4.came_near_ref.refs_2_ = f32[136,128]{1,0:T(8,128)S(1)} collective-permute-done((f32[136,128]{1,0:T(8,128)S(1)}, f32[136,128]{1,0:T(8,128)S(1)}, u32[]{:S(2)}, u32[]{:S(2)}) %collective-permute-start.4) | collective-permute-done | bytes 69664 | tf_op jit(solution)/shard_map/ppermute | solution.py:361
  41.5 2.9 %inverse.6.inv_ref.refs_0_ = f32[128,128]{1,0:T(8,128)S(1)} custom-call(f32[136,128]{1,0:T(8,128)S(1)} %near.4.near_ref.refs_5_.refs_1_, f32[136,128]{1,0:T(8,128)S(1)} %collective-permute-done.4.came_near_ref.refs_2_), custom_call_target="tpu_custom_call" | custom-call | flops 6291456000 | bytes 196608 | tf_op jit(solution)/shard_map/inverse/pallas_call | solution.py:366
  44.5 0.0 collective-permute-done.5.came_far_ref.refs_4_
  44.5 0.6 near.5.near_ref.refs_5_.refs_1_
  45.1 1.7 %collective-permute-start.6 = (f32[136,128]{1,0:T(8,128)S(1)}, f32[136,128]{1,0:T(8,128)S(1)}, u32[]{:S(2)}, u32[]{:S(2)}) collective-permute-start(f32[136,128]{1,0:T(8,128)S(1)} %near.5.near_ref.refs_5_.refs_1_), channel_id=1, source_target_pairs={{0,8},{1,9},{2,10},{3,11},{4,12},{5,13},{6,14},{7,15},{8,0},{9,1},... | collective-permute-start | bytes 208904 | tf_op jit(solution)/shard_map/ppermute | solution.py:361
  46.8 0.8 %far.5 = (f32[264,128]{1,0:T(8,128)S(1)}, f32[264,128]{1,0:T(8,128)S(1)}) custom-call(f32[128,128]{1,0:T(8,128)S(1)} %inverse.6.inv_ref.refs_0_, f32[136,128]{1,0:T(8,128)S(1)} %near.4.near_ref.refs_5_.refs_1_, f32[136,128]{1,0:T(8,128)S(1)} %collective-permute-done.4.came_near_ref.refs_2_, f32[264,128]{1,0:T(8,128)S(1)} %get-tuple-element.20.far_ref.refs_3_, ...), custom_call_target="tpu_custom_call" | custom-call | flops 1468006400 | bytes 196608 | tf_op jit(solution)/shard_map/far/pallas_call | solution.py:366
  47.6 0.5 collective-permute-start.7
  48.1 1.8 %collective-permute-done.6.came_near_ref.refs_2_ = f32[136,128]{1,0:T(8,128)S(1)} collective-permute-done((f32[136,128]{1,0:T(8,128)S(1)}, f32[136,128]{1,0:T(8,128)S(1)}, u32[]{:S(2)}, u32[]{:S(2)}) %collective-permute-start.6) | collective-permute-done | bytes 69664 | tf_op jit(solution)/shard_map/ppermute | solution.py:361
  49.8 3.2 %inverse.7.refs_0_ = f32[128,128]{1,0:T(8,128)S(1)} custom-call(f32[136,128]{1,0:T(8,128)S(1)} %near.5.near_ref.refs_5_.refs_1_, f32[136,128]{1,0:T(8,128)S(1)} %collective-permute-done.6.came_near_ref.refs_2_), custom_call_target="tpu_custom_call" | custom-call | flops 6291456000 | bytes 196608 | tf_op jit(solution)/shard_map/inverse/pallas_call | solution.py:366
  53.0 0.0 copy-start
  53.0 0.0 collective-permute-done.7.refs_4_
  53.0 4.3 %closing.1 = (f32[136,128]{1,0:T(8,128)S(1)}, f32[264,128]{1,0:T(8,128)S(1)}, f32[136,128]{1,0:T(8,128)S(1)}) custom-call(f32[128,128]{1,0:T(8,128)S(1)} %inverse.7.refs_0_, f32[136,128]{1,0:T(8,128)S(1)} %near.5.near_ref.refs_5_.refs_1_, f32[136,128]{1,0:T(8,128)S(1)} %collective-permute-done.6.came_near_ref.refs_2_, ...), custom_call_target="tpu_custom_call" | custom-call | flops 4194304000 | bytes 196608 | tf_op jit(solution)/shard_map/closing/pallas_call | solution.py:366
  57.3 2.7 %collective-permute-start.8 = (f32[136,128]{1,0:T(8,128)S(1)}, f32[136,128]{1,0:T(8,128)S(1)}, u32[]{:S(2)}, u32[]{:S(2)}) collective-permute-start(f32[136,128]{1,0:T(8,128)S(1)} %get-tuple-element.22.refs_0_), channel_id=1, source_target_pairs={{0,16},{1,17},{2,18},{3,19},{4,20},{5,21},{6,22},{7,23},{8,24},{9,... | collective-permute-start | bytes 208904 | tf_op jit(solution)/shard_map/ppermute | solution.py:361
  60.0 2.6 %collective-permute-done.8.refs_1_ = f32[136,128]{1,0:T(8,128)S(1)} collective-permute-done((f32[136,128]{1,0:T(8,128)S(1)}, f32[136,128]{1,0:T(8,128)S(1)}, u32[]{:S(2)}, u32[]{:S(2)}) %collective-permute-start.8) | collective-permute-done | bytes 69664 | tf_op jit(solution)/shard_map/ppermute | solution.py:361
  62.6 0.0 copy-done
  62.6 5.2 %final.1 = f32[8,128]{1,0:T(8,128)} custom-call(f32[136,128]{1,0:T(8,128)S(1)} %get-tuple-element.22.refs_0_, f32[136,128]{1,0:T(8,128)S(1)} %collective-permute-done.8.refs_1_, f32[264,128]{1,0:T(8,128)S(1)} %get-tuple-element.23.refs_2_, f32[264,128]{1,0:T(8,128)S(1)} %get-tuple-element.24.refs_3_, f32[264,128]{1,0:T(8,128)S(1)} %get-tuple-element.25.refs_4_, ...), custom_call_target="tpu_custom_call" | custom-call | tf_op jit(solution)/shard_map/final/pallas_call | solution.py:394
Async XLA Ops:
  20.7 1.6 %collective-permute-start = (f32[136,128]{1,0:T(8,128)}, f32[136,128]{1,0:T(8,128)S(1)}, u32[]{:S(2)}, u32[]{:S(2)}) collective-permute-start(f32[136,128]{1,0:T(8,128)} %get-tuple-element.17.near_ref.refs_1_), channel_id=1, source_target_pairs={{0,1},{1,0},{2,3},{3,2},{4,5},{5,4},{6,7},{7,6},{8,9},{9,8},{10,11... | collective-permute-start | bytes 208904 | tf_op jit(solution)/shard_map/ppermute | solution.py:361
  21.2 5.0 %copy-start.1 = (f32[264,128]{1,0:T(8,128)S(1)}, f32[264,128]{1,0:T(8,128)}, u32[]{:S(2)}) copy-start(f32[264,128]{1,0:T(8,128)} %get-tuple-element.18.far_ref.refs_3_) | copy-start | bytes 405508
  21.2 4.9 %collective-permute-start.1 = (f32[264,128]{1,0:T(8,128)}, f32[264,128]{1,0:T(8,128)S(1)}, u32[]{:S(2)}, u32[]{:S(2)}) collective-permute-start(f32[264,128]{1,0:T(8,128)} %get-tuple-element.18.far_ref.refs_3_), channel_id=1, source_target_pairs={{0,1},{1,0},{2,3},{3,2},{4,5},{5,4},{6,7},{7,6},{8,9},{9,8},{10,11... | collective-permute-start | bytes 405512 | tf_op jit(solution)/shard_map/ppermute | solution.py:361
  22.3 0.9 %copy-start.2 = (f32[136,128]{1,0:T(8,128)S(1)}, f32[136,128]{1,0:T(8,128)}, u32[]{:S(2)}) copy-start(f32[136,128]{1,0:T(8,128)} %get-tuple-element.17.near_ref.refs_1_) | copy-start | bytes 208900
  26.8 5.4 %collective-permute-start.2 = (f32[136,128]{1,0:T(8,128)S(1)}, f32[136,128]{1,0:T(8,128)S(1)}, u32[]{:S(2)}, u32[]{:S(2)}) collective-permute-start(f32[136,128]{1,0:T(8,128)S(1)} %near.3.near_ref.refs_5_.refs_1_), channel_id=1, source_target_pairs={{0,2},{1,3},{2,0},{3,1},{4,6},{5,7},{6,4},{7,5},{8,10},{9,11},{10,... | collective-permute-start | bytes 208904 | tf_op jit(solution)/shard_map/ppermute | solution.py:361
  30.5 5.4 %collective-permute-start.3 = (f32[264,128]{1,0:T(8,128)S(1)}, f32[264,128]{1,0:T(8,128)S(1)}, u32[]{:S(2)}, u32[]{:S(2)}) collective-permute-start(f32[264,128]{1,0:T(8,128)S(1)} %get-tuple-element.19.far_ref.refs_3_), channel_id=1, source_target_pairs={{0,2},{1,3},{2,0},{3,1},{4,6},{5,7},{6,4},{7,5},{8,10},{9,11},{10,... | collective-permute-start | bytes 405512 | tf_op jit(solution)/shard_map/ppermute | solution.py:361
  36.5 5.0 %collective-permute-start.4 = (f32[136,128]{1,0:T(8,128)S(1)}, f32[136,128]{1,0:T(8,128)S(1)}, u32[]{:S(2)}, u32[]{:S(2)}) collective-permute-start(f32[136,128]{1,0:T(8,128)S(1)} %near.4.near_ref.refs_5_.refs_1_), channel_id=1, source_target_pairs={{0,4},{1,5},{2,6},{3,7},{4,0},{5,1},{6,2},{7,3},{8,12},{9,13},{10,... | collective-permute-start | bytes 208904 | tf_op jit(solution)/shard_map/ppermute | solution.py:361
  38.9 5.6 %collective-permute-start.5 = (f32[264,128]{1,0:T(8,128)S(1)}, f32[264,128]{1,0:T(8,128)S(1)}, u32[]{:S(2)}, u32[]{:S(2)}) collective-permute-start(f32[264,128]{1,0:T(8,128)S(1)} %get-tuple-element.20.far_ref.refs_3_), channel_id=1, source_target_pairs={{0,4},{1,5},{2,6},{3,7},{4,0},{5,1},{6,2},{7,3},{8,12},{9,13},{10,... | collective-permute-start | bytes 405512 | tf_op jit(solution)/shard_map/ppermute | solution.py:361
  45.1 4.7 %collective-permute-start.6 = (f32[136,128]{1,0:T(8,128)S(1)}, f32[136,128]{1,0:T(8,128)S(1)}, u32[]{:S(2)}, u32[]{:S(2)}) collective-permute-start(f32[136,128]{1,0:T(8,128)S(1)} %near.5.near_ref.refs_5_.refs_1_), channel_id=1, source_target_pairs={{0,8},{1,9},{2,10},{3,11},{4,12},{5,13},{6,14},{7,15},{8,0},{9,1},... | collective-permute-start | bytes 208904 | tf_op jit(solution)/shard_map/ppermute | solution.py:361
  47.6 5.5 %collective-permute-start.7 = (f32[264,128]{1,0:T(8,128)S(1)}, f32[264,128]{1,0:T(8,128)S(1)}, u32[]{:S(2)}, u32[]{:S(2)}) collective-permute-start(f32[264,128]{1,0:T(8,128)S(1)} %get-tuple-element.21.refs_3_), channel_id=1, source_target_pairs={{0,8},{1,9},{2,10},{3,11},{4,12},{5,13},{6,14},{7,15},{8,0},{9,1},... | collective-permute-start | bytes 405512 | tf_op jit(solution)/shard_map/ppermute | solution.py:361
  53.0 9.6 %copy-start = (f32[7,264,128]{2,1,0:T(8,128)S(1)}, f32[7,264,128]{2,1,0:T(8,128)}, u32[]{:S(2)}) copy-start(f32[7,264,128]{2,1,0:T(8,128)} %get-tuple-element.28.refs_7_) | copy-start | bytes 2838532
  57.3 5.3 %collective-permute-start.8 = (f32[136,128]{1,0:T(8,128)S(1)}, f32[136,128]{1,0:T(8,128)S(1)}, u32[]{:S(2)}, u32[]{:S(2)}) collective-permute-start(f32[136,128]{1,0:T(8,128)S(1)} %get-tuple-element.22.refs_0_), channel_id=1, source_target_pairs={{0,16},{1,17},{2,18},{3,19},{4,20},{5,21},{6,22},{7,23},{8,24},{9,... | collective-permute-start | bytes 208904 | tf_op jit(solution)/shard_map/ppermute | solution.py:361
